TPU v7x, 512 devices: a whole 4x4x16 slice. The times are simulated.
512 devices in a mesh: fsdp: 32 (over z, x_lo), tensor: 16 (over y, x_hi, core).
Axes of the slice: x: 4 (x_hi: 2, x_lo: 2; x = x_hi * 2 + x_lo), y: 4, z: 16, core: 2. Of those that a mesh axis runs over, the one named last changes fastest.
Arguments:
- tokens: bfloat16 [65536, 3072], P(('fsdp', 'tensor')), may hold values from -6 to 6
- positions: int32 [65536], P(('fsdp', 'tensor')), may hold values from 0 to 4095
- key_weight: bfloat16 [3072, 48, 128], P('fsdp', 'tensor'), may hold values from -0.109375 to 0.109375
- key_bias: bfloat16 [48, 128], P('tensor'), may hold values from -3 to 3
- conv_taps: float32 [48, 3, 128], P('tensor'), may hold values from -3 to 3
Outputs:
- keys_out: bfloat16 [65536, 48, 128], P('fsdp', 'tensor')
All inputs are finite; a program needn't handle non-finite values.
Results may differ from a plain program's by a relative error of at most 0.001.
Values may be sent and summed in bfloat16 or wider, within the bound.
No kernel may reach another device: no remote copies, remote signals or barrier semaphores. Data moves between devices by JAX's collectives and lax.ppermute only.
A program may use at most 64 MiB of HBM per device.

v0:
```python
import jax
import jax.numpy as jnp
from jax import lax
from jax.sharding import PartitionSpec as P

HEAD_DIM = 128


rope_base = 10000.0


def finish(projected, places, key_bias, conv_taps, seq_len):
    row_count = projected.shape[0]
    head_count = key_bias.shape[0]
    projected = (
        projected.reshape(row_count // seq_len, seq_len, head_count, HEAD_DIM)
        + key_bias.astype(jnp.float32)[None, None]
    )
    zero_row = jnp.zeros((row_count // seq_len, 1, head_count, HEAD_DIM), jnp.float32)
    previous_one = jnp.concatenate([zero_row, projected[:, :-1]], axis=1)
    previous_two = jnp.concatenate([zero_row, previous_one[:, :-1]], axis=1)
    convolved = (
        conv_taps[None, None, :, 0] * projected
        + conv_taps[None, None, :, 1] * previous_one
        + conv_taps[None, None, :, 2] * previous_two
    )
    convolved = convolved.reshape(row_count, head_count, HEAD_DIM)
    half_dim = HEAD_DIM // 2
    inv_freq = rope_base ** (-(jnp.arange(half_dim, dtype=jnp.float32) * 2.0) / HEAD_DIM)
    angles = places.astype(jnp.float32)[:, None] * inv_freq[None, :]
    cosine = jnp.cos(angles)[:, None, :]
    sine = jnp.sin(angles)[:, None, :]
    first_half = convolved[..., :half_dim]
    second_half = convolved[..., half_dim:]
    new_first = first_half * cosine - second_half * sine
    new_second = second_half * cosine + first_half * sine
    result = jnp.concatenate([new_first, new_second], axis=-1)
    return result.astype(jnp.bfloat16)


def body(tokens, positions, key_weight, key_bias, conv_taps):
    columns = key_weight.shape[1] * key_weight.shape[2]
    seq_tokens, places = (
        lax.all_gather(tokens, "tensor", axis=0, tiled=True),
        lax.all_gather(positions, "tensor", axis=0, tiled=True),
    )
    weight_piece = lax.all_gather(key_weight, "fsdp", axis=0, tiled=True)
    piece_rows = weight_piece.shape[0]
    projected = jnp.dot(
        seq_tokens, weight_piece.reshape(piece_rows, columns), preferred_element_type=jnp.float32
    )
    seq_length = projected.shape[0] // 2
    return finish(projected, places, key_bias, conv_taps, seq_length)


def solution(mesh):
    return jax.shard_map(
        body,
        mesh=mesh,
        in_specs=(
            P(("fsdp", "tensor"), None),
            P(("fsdp", "tensor")),
            P("fsdp", "tensor", None),
            P("tensor", None),
            P("tensor", None, None),
        ),
        out_specs=P("fsdp", "tensor", None),
        check_vma=False,
    )
```

profile of v0, /device:TPU:1, one launch (start us, length us, event | category | flops | bytes accessed | tf_op | source)
XLA Modules:
  0.0 280.0 jit_solution(18154842430025373095)
XLA Ops:
  6.5 0.0 all-gather.6.cloned.1.call-start
  6.5 0.7 all-gather.6.cloned.1.call-update
  7.3 0.0 all-gather.4.cloned.1.call-start
  7.3 0.7 all-gather.4.cloned.1.call-update
  8.0 0.7 convert_element_type.7
  8.7 0.8 fusion.5
  9.5 25.8 %all-gather = s32[16,1,128]{2,1,0:T(1,128)S(1)} all-gather(s32[1,1,128]{2,1,0:T(1,128)} %bitcast.33), channel_id=1, replica_groups=mesh['fsdp'=32,'tensor'=16] {'tensor'}, dimensions={0}, use_global_device_ids=true | all-gather | bytes 8704 | tf_op jit(solution)/shard_map/all_gather | solution.py:45
  35.3 3.7 %multiply_cosine_fusion = (f32[2048,64]{1,0:T(8,128)S(1)}, f32[2048,64]{1,0:T(8,128)S(1)}) fusion(f32[64]{0:T(128)S(1)} %multiply_power_fusion, f32[2048]{0:T(1024)S(1)} %bitcast.31), kind=kLoop, calls=%fused_computation.9 | loop fusion | flops 131072 | bytes 1057024 | tf_op jit(solution)/shard_map/cos | solution.py:31
  39.0 90.4 %all-gather.6.cloned.1.call-done = bf16[3072,3,128]{2,0,1:T(8,128)(2,1)} async-done(((bf16[96,3,128]{2,0,1:T(8,128)(2,1)}), bf16[3072,3,128]{2,0,1:T(8,128)(2,1)}) %all-gather.6.cloned.1.call-update) | async-done | bytes 2359312 | tf_op jit(solution)/shard_map/all_gather | solution.py:47
  129.4 4.3 %copy.8 = bf16[3072,3,128]{0,2,1:T(8,128)(2,1)} copy(bf16[3072,3,128]{2,0,1:T(8,128)(2,1)} %all-gather.6.cloned.1.call-done) | data formatting | bytes 4718592 | tf_op jit(solution)/shard_map/all_gather | solution.py:47
  133.6 124.5 %all-gather.4.cloned.1.call-done = bf16[2048,3072]{1,0:T(8,128)(2,1)} async-done(((bf16[128,3072]{1,0:T(8,128)(2,1)}), bf16[2048,3072]{1,0:T(8,128)(2,1)}) %all-gather.4.cloned.1.call-update) | async-done | bytes 12582928 | tf_op jit(solution)/shard_map/all_gather | solution.py:44
  258.1 10.5 %fusion.2 = f32[2,1024,3,128]{3,1,2,0:T(8,128)S(1)} fusion(bf16[2,1024,3072,1]{2,1,3,0:T(8,128)(2,1)} %bitcast.34, bf16[3072,3,128]{0,2,1:T(8,128)(2,1)} %copy.8, f32[3,128]{1,0:T(4,128)S(1)} %convert_element_type.7), kind=kOutput, calls=%fused_computation.6 | convolution fusion | flops 4832624640 | bytes 18089472 | tf_op jit(solution)/shard_map/dot_general | solution.py:49
  268.7 0.2 pad_slice_fusion
  268.9 0.9 multiply_add_fusion
  269.8 0.2 copy.9
  270.0 1.1 subtract_convert_fusion
  271.2 2.0 pad_maximum_fusion
  (4 shorter events, 0.0 us)
Async XLA Ops:
  6.5 122.8 %all-gather.6.cloned.1.call-start = ((), (), s32[]{:S(2)}) async-start(), calls=%async_computation.1 | async-start | bytes 2433024 | tf_op jit(solution)/shard_map/all_gather | solution.py:47
  7.3 250.8 %all-gather.4.cloned.1.call-start = ((), (), s32[]{:S(2)}) async-start(), calls=%async_computation | async-start | bytes 13369344 | tf_op jit(solution)/shard_map/all_gather | solution.py:44
Sparse Core Ops, SparseCore 0:
  9.4 119.8 all-gather.5
  132.7 125.3 all-gather.3
where the time goes:
time: 280 us
  waiting for transfers between devices  216 us (77%)
  blocking collectives  25.8 us (9%)
  between operations  13.5 us (5%)
  matrix products  10.5 us (4%)
  other arithmetic  8.46 us (3%)
  local copies, waits for them, and re-layouts  5.51 us (2%)
    all_gather x1, waiting for transfers between devices, body(): lax.all_gather(tokens, 'tensor', axis=0, tiled=True)  124 us
    all_gather x1, waiting for transfers between devices, body(): weight_piece = lax.all_gather(key_weight, 'fsdp', axis=0, tiled=True)  90.4 us
    all_gather x1, blocking collectives, body(): lax.all_gather(positions, 'tensor', axis=0, tiled=True)  25.8 us
    dot_general x1, matrix products, body(): jnp.dot(seq_tokens, weight_piece.reshape(piece_rows, columns), preferred_...  10.5 us
  transfers between devices with their start and end apart: 2, of which 2 were waited for; matrix products, arithmetic and copies ran while one was open for 3% of the time, Pallas kernels for 0%

commit v1 on v0

v1 whole, which is shorter than its diff:
```python
import jax
import jax.numpy as jnp
from jax import lax
from jax.experimental import pallas as pl
from jax.experimental.pallas import tpu as pltpu
from jax.sharding import PartitionSpec as P

HEAD_DIM = 128
SEQ_LEN = 1024
rope_base = 10000.0

Y, X_HI, CORE = 4, 2, 2
BATCH = 4


def keys_kernel(shards, rows, place_ref, *refs):
    token_refs = refs[:shards]
    w_ref, bias_ref, taps_ref, cos_ref, sin_ref, out_ref, held, w_flat, proj, sems = refs[shards:]
    copies = [pltpu.make_async_copy(token_refs[i], held.at[i], sems.at[i]) for i in range(shards)]
    for copy in copies:
        copy.start()
    heads = out_ref.shape[0]
    piece_rows = w_ref.shape[1] // heads
    for piece in range(w_ref.shape[0]):
        for head in range(heads):
            w_flat[piece * piece_rows : (piece + 1) * piece_rows, head * HEAD_DIM : (head + 1) * HEAD_DIM] = w_ref[
                piece, head * piece_rows : (head + 1) * piece_rows, :
            ]
    proj[0:8, :] = jnp.zeros((8, proj.shape[1]), jnp.float32)
    for first in range(0, shards, BATCH):
        for copy in copies[first : first + BATCH]:
            copy.wait()
        block = held[first : first + BATCH].reshape(BATCH * rows, held.shape[2])
        raw = jnp.dot(block, w_flat[...], preferred_element_type=jnp.float32) + bias_ref[...]
        for i in range(BATCH):
            start = pl.multiple_of(place_ref[first + i] * rows + 8, 8)
            proj[pl.ds(start, rows), :] = raw[i * rows : (i + 1) * rows]

    @pl.loop(0, shards)
    def _(shard):
        start = pl.multiple_of(shard * rows, rows)
        tail = proj[pl.ds(start, 8), :]
        tail = jnp.where(lax.rem(shard, SEQ_LEN // rows) == 0, 0.0, tail)
        cosine = cos_ref[pl.ds(start, rows), :]
        sine = sin_ref[pl.ds(start, rows), :]
        row = lax.broadcasted_iota(jnp.int32, (rows, HEAD_DIM), 0)
        for head in range(heads):
            lanes = slice(head * HEAD_DIM, (head + 1) * HEAD_DIM)
            now = proj[pl.ds(start + 8, rows), lanes]
            before_one, before_two = tail[7:8, lanes], tail[6:7, lanes]
            previous_one = jnp.where(row == 0, before_one, pltpu.roll(now, 1, 0))
            previous_two = jnp.where(row == 0, before_two, jnp.where(row == 1, before_one, pltpu.roll(now, 2, 0)))
            part = taps_ref[0:1, lanes] * now + taps_ref[1:2, lanes] * previous_one + taps_ref[2:3, lanes] * previous_two
            turned = part * cosine + pltpu.roll(part, HEAD_DIM // 2, 1) * sine
            out_ref[head, pl.ds(start, rows), :] = turned.astype(out_ref.dtype)


def rotation(places):
    half_dim = HEAD_DIM // 2
    inv_freq = rope_base ** (-(jnp.arange(half_dim, dtype=jnp.float32) * 2.0) / HEAD_DIM)
    angles = places.astype(jnp.float32)[:, None] * inv_freq[None, :]
    cosine = jnp.cos(angles)
    sine = jnp.sin(angles)
    return jnp.concatenate([cosine, cosine], axis=1), jnp.concatenate([-sine, sine], axis=1)


def shifted(y_step, x_step, core_step):
    pairs = []
    for y in range(Y):
        for x in range(X_HI):
            for c in range(CORE):
                there = (((y + y_step) % Y) * X_HI + (x + x_step) % X_HI) * CORE + (c + core_step) % CORE
                pairs.append(((y * X_HI + x) * CORE + c, there))
    return pairs


def body(fsdp, tensor, tokens, positions, key_weight, key_bias, conv_taps):
    rows, depth = tokens.shape
    piece, heads, _ = key_weight.shape
    columns = heads * HEAD_DIM

    own_weight = jnp.transpose(key_weight, (1, 0, 2))
    near_weight = lax.ppermute(own_weight, "fsdp", [(i, i ^ 1) for i in range(fsdp)])
    is_low = lax.axis_index("fsdp") % 2 == 0
    first = jnp.where(is_low, own_weight, near_weight)
    second = jnp.where(is_low, near_weight, own_weight)
    pair = jnp.concatenate([first, second], axis=1).reshape(heads * 2 * piece, HEAD_DIM)
    line_groups = [[2 * i + j for i in range(fsdp // 2)] for j in range(2)]
    weight = lax.all_gather(pair, "fsdp", axis=0, axis_index_groups=line_groups)

    tokens, positions, pair = lax.optimization_barrier((tokens, positions, pair))
    me = lax.axis_index("tensor")
    my_y, my_x, my_core = me // (X_HI * CORE), me // CORE % X_HI, me % CORE
    blocks, places_of = [], []
    for x_step in range(X_HI):
        for y_step in (0, 1, 3, 2):
            block = tokens if x_step == 0 and y_step == 0 else lax.ppermute(tokens, "tensor", shifted(y_step, x_step, 0))
            blocks.append(block)
            places_of.append(((my_y + Y - y_step) % Y) * X_HI + (my_x + x_step) % X_HI)
    across = [lax.ppermute(block, "tensor", shifted(0, 0, 1)) for block in blocks]
    place = jnp.stack([p * CORE + my_core for p in places_of] + [p * CORE + 1 - my_core for p in places_of])

    places = lax.all_gather(positions, "tensor", axis=0, tiled=True)
    cosine, sine = rotation(places)

    taps = jnp.transpose(conv_taps, (1, 0, 2)).reshape(conv_taps.shape[1], columns)
    bias = key_bias.astype(jnp.float32).reshape(1, columns)
    total = rows * tensor
    vmem = pl.BlockSpec(memory_space=pltpu.VMEM)
    keys = pl.pallas_call(
        lambda *refs: keys_kernel(tensor, rows, *refs),
        in_specs=[pl.BlockSpec(memory_space=pltpu.SMEM)] + [pl.BlockSpec(memory_space=pl.ANY)] * tensor + [vmem] * 5,
        out_specs=vmem,
        out_shape=jax.ShapeDtypeStruct((heads, total, HEAD_DIM), jnp.bfloat16),
        scratch_shapes=[
            pltpu.VMEM((tensor, rows, depth), jnp.bfloat16),
            pltpu.VMEM((depth, columns), jnp.bfloat16),
            pltpu.VMEM((total + 8, columns), jnp.float32),
            pltpu.SemaphoreType.DMA((tensor,)),
        ],
        compiler_params=pltpu.CompilerParams(vmem_limit_bytes=56 * 1024 * 1024),
        cost_estimate=pl.CostEstimate(
            flops=2 * total * depth * columns,
            bytes_accessed=2 * (total * depth + depth * columns + total * columns),
            transcendentals=0,
        ),
    )(place, *blocks, *across, weight, bias, taps, cosine, sine)
    return jnp.transpose(keys, (1, 0, 2))


def solution(mesh):
    fsdp, tensor = mesh.shape["fsdp"], mesh.shape["tensor"]
    return jax.shard_map(
        lambda *args: body(fsdp, tensor, *args),
        mesh=mesh,
        in_specs=(
            P(("fsdp", "tensor"), None),
            P(("fsdp", "tensor")),
            P("fsdp", "tensor", None),
            P("tensor", None),
            P("tensor", None, None),
        ),
        out_specs=P("fsdp", "tensor", None),
        check_vma=False,
    )
```

time: 280 us -> 164 us (0.59)
  waiting for transfers between devices: 216 us -> 34.2 us
  starting transfers between devices: 0.04 us -> 63.3 us
  Pallas kernels: 0 us -> 14.8 us
  matrix products: 10.5 us -> 0 us
    all_gather x2 -> x1, waiting for transfers between devices: 215 us -> 0.01 us  [body(): weight = lax.all_gather(pair, 'fsdp', axis=0, axis_index_groups=line_groups)]
    ppermute x0 -> x16, starting transfers between devices: none -> 63.3 us  [the longest x8 31.6 us: body(): lax.ppermute(block, 'tensor', shifted(0, 0, 1))]
    ppermute x0 -> x16, waiting for transfers between devices: none -> 34.2 us  [the longest x7 32.3 us: body(): lax.ppermute(tokens, 'tensor', shifted(y_step, x_step, 0))]
    pallas_call x0 -> x1, Pallas kernels: none -> 14.8 us  [body(): pl.pallas_call(lambda *refs: keys_kernel(tensor, rows, *refs), in_specs=[...]
    dot_general x1 -> x0, matrix products: 10.5 us -> none  [body(): jnp.dot(seq_tokens, weight_piece.reshape(piece_rows, columns), preferred_...]
    all_gather x1 -> x0, local copies, waits for them, and re-layouts: 4.28 us -> none  [body(): weight_piece = lax.all_gather(key_weight, 'fsdp', axis=0, tiled=True)]
    unnamed x2 -> x17, local copies, waits for them, and re-layouts: 0.01 us -> 4.18 us
    neg x0 -> x1, other arithmetic: none -> 3.72 us  [rotation(): -sine]
  transfers between devices with their start and end apart: 2 -> 17, of which waited for: 2 -> 5; matrix products, arithmetic and copies ran while one was open for 3% -> 5% of each run, Pallas kernels for 0% -> 0%
where the time goes in v1:
time: 164 us; the launch traced here: 163 us
  starting transfers between devices  63.3 us (39%)
  waiting for transfers between devices  34.2 us (21%)
  blocking collectives  24.5 us (15%)
  Pallas kernels  14.8 us (9%)
  between operations  13.8 us (8%)
  other arithmetic  7.94 us (5%)
  local copies, waits for them, and re-layouts  4.79 us (3%)
    ppermute x7, waiting for transfers between devices, body(): lax.ppermute(tokens, 'tensor', shifted(y_step, x_step, 0))  32.3 us
    ppermute x8, starting transfers between devices, body(): lax.ppermute(block, 'tensor', shifted(0, 0, 1))  31.6 us
    ppermute x7, starting transfers between devices, body(): lax.ppermute(tokens, 'tensor', shifted(y_step, x_step, 0))  27.7 us
    all_gather x1, blocking collectives, body(): places = lax.all_gather(positions, 'tensor', axis=0, tiled=True)  24.5 us
    pallas_call x1, Pallas kernels, body(): pl.pallas_call(lambda *refs: keys_kernel(tensor, rows, *refs), in_specs=[...  14.8 us
    unnamed x17, local copies, waits for them, and re-layouts  4.18 us
    ppermute x1, starting transfers between devices, body(): lax.ppermute(own_weight, 'fsdp', [(i, i ^ 1) for i in range(fsdp)])  3.94 us
    neg x1, other arithmetic, rotation(): -sine  3.72 us
  transfers between devices with their start and end apart: 17, of which 5 were waited for; matrix products, arithmetic and copies ran while one was open for 5% of the time, Pallas kernels for 0%

profile of v1, /device:TPU:1, one launch (start us, length us, event | category | flops | bytes accessed | tf_op | source)
XLA Modules:
  0.0 163.3 jit_solution(2709889701860848990)
XLA Ops:
  6.5 3.9 %collective-permute-start.15 = (bf16[3,96,128]{2,1,0:T(8,128)(2,1)}, bf16[3,96,128]{2,1,0:T(8,128)(2,1)S(1)}, u32[]{:S(2)}, u32[]{:S(2)}) collective-permute-start(bf16[3,96,128]{2,1,0:T(8,128)(2,1)} %bitcast.33), channel_id=1, source_target_pairs={{0,16},{16,0},{32,48},{48,32},{64,80},{80,64},{96,112},{112,96},{1... | collective-permute-start | bytes 221192 | tf_op jit(solution)/shard_map/ppermute | solution.py:83
  10.5 1.9 %collective-permute-done.15 = bf16[3,96,128]{2,1,0:T(8,128)(2,1)S(1)} collective-permute-done((bf16[3,96,128]{2,1,0:T(8,128)(2,1)}, bf16[3,96,128]{2,1,0:T(8,128)(2,1)S(1)}, u32[]{:S(2)}, u32[]{:S(2)}) %collective-permute-start.15) | collective-permute-done | bytes 73760 | tf_op jit(solution)/shard_map/ppermute | solution.py:83
  14.0 5.1 %collective-permute-start.2 = (bf16[128,3072]{1,0:T(8,128)(2,1)}, bf16[128,3072]{1,0:T(8,128)(2,1)S(1)}, u32[]{:S(2)}, u32[]{:S(2)}) collective-permute-start(bf16[128,3072]{1,0:T(8,128)(2,1)} %refs_1_), channel_id=1, source_target_pairs={{0,8},{1,9},{2,10},{3,11},{4,12},{5,13},{6,14},{7,15},{8,0},{9,1},... | collective-permute-start | bytes 2359304 | tf_op jit(solution)/shard_map/ppermute | solution.py:97
  19.1 4.7 %collective-permute-start.3 = (bf16[128,3072]{1,0:T(8,128)(2,1)}, bf16[128,3072]{1,0:T(8,128)(2,1)S(1)}, u32[]{:S(2)}, u32[]{:S(2)}) collective-permute-start(bf16[128,3072]{1,0:T(8,128)(2,1)} %refs_1_), channel_id=1, source_target_pairs={{0,2},{1,3},{2,0},{3,1},{4,6},{5,7},{6,4},{7,5},{8,10},{9,11},{10,... | collective-permute-start | bytes 2359304 | tf_op jit(solution)/shard_map/ppermute | solution.py:97
  23.8 2.3 %collective-permute-start.4 = (bf16[128,3072]{1,0:T(8,128)(2,1)}, bf16[128,3072]{1,0:T(8,128)(2,1)S(1)}, u32[]{:S(2)}, u32[]{:S(2)}) collective-permute-start(bf16[128,3072]{1,0:T(8,128)(2,1)} %refs_1_), channel_id=1, source_target_pairs={{0,6},{1,7},{2,4},{3,5},{4,10},{5,11},{6,8},{7,9},{8,14},{9,15},{1... | collective-permute-start | bytes 2359304 | tf_op jit(solution)/shard_map/ppermute | solution.py:97
  26.0 6.7 %collective-permute-start.5 = (bf16[128,3072]{1,0:T(8,128)(2,1)}, bf16[128,3072]{1,0:T(8,128)(2,1)S(1)}, u32[]{:S(2)}, u32[]{:S(2)}) collective-permute-start(bf16[128,3072]{1,0:T(8,128)(2,1)} %refs_1_), channel_id=1, source_target_pairs={{0,14},{1,15},{2,12},{3,13},{4,2},{5,3},{6,0},{7,1},{8,6},{9,7},{1... | collective-permute-start | bytes 2359304 | tf_op jit(solution)/shard_map/ppermute | solution.py:97
  32.7 1.9 %collective-permute-start.6 = (bf16[128,3072]{1,0:T(8,128)(2,1)}, bf16[128,3072]{1,0:T(8,128)(2,1)}, u32[]{:S(2)}, u32[]{:S(2)}) collective-permute-start(bf16[128,3072]{1,0:T(8,128)(2,1)} %refs_1_), channel_id=1, source_target_pairs={{0,10},{1,11},{2,8},{3,9},{4,14},{5,15},{6,12},{7,13},{8,2},{9,3},... | collective-permute-start | bytes 2359304 | tf_op jit(solution)/shard_map/ppermute | solution.py:97
  34.6 3.7 %collective-permute-start = (bf16[128,3072]{1,0:T(8,128)(2,1)}, bf16[128,3072]{1,0:T(8,128)(2,1)}, u32[]{:S(2)}, u32[]{:S(2)}) collective-permute-start(bf16[128,3072]{1,0:T(8,128)(2,1)} %refs_1_), channel_id=1, source_target_pairs={{0,4},{1,5},{2,6},{3,7},{4,8},{5,9},{6,10},{7,11},{8,12},{9,13},{1... | collective-permute-start | bytes 2359304 | tf_op jit(solution)/shard_map/ppermute | solution.py:97
  38.8 3.5 %collective-permute-start.1 = (bf16[128,3072]{1,0:T(8,128)(2,1)}, bf16[128,3072]{1,0:T(8,128)(2,1)}, u32[]{:S(2)}, u32[]{:S(2)}) collective-permute-start(bf16[128,3072]{1,0:T(8,128)(2,1)} %refs_1_), channel_id=1, source_target_pairs={{0,12},{1,13},{2,14},{3,15},{4,0},{5,1},{6,2},{7,3},{8,4},{9,5},{1... | collective-permute-start | bytes 2359304 | tf_op jit(solution)/shard_map/ppermute | solution.py:97
  42.3 14.7 %collective-permute-done.4.refs_6_ = bf16[128,3072]{1,0:T(8,128)(2,1)S(1)} collective-permute-done((bf16[128,3072]{1,0:T(8,128)(2,1)}, bf16[128,3072]{1,0:T(8,128)(2,1)S(1)}, u32[]{:S(2)}, u32[]{:S(2)}) %collective-permute-start.4) | collective-permute-done | bytes 786464 | tf_op jit(solution)/shard_map/ppermute | solution.py:97
  57.0 7.6 %collective-permute-start.7 = (bf16[128,3072]{1,0:T(8,128)(2,1)}, bf16[128,3072]{1,0:T(8,128)(2,1)}, u32[]{:S(2)}, u32[]{:S(2)}) collective-permute-start(bf16[128,3072]{1,0:T(8,128)(2,1)} %refs_1_), channel_id=1, source_target_pairs={{0,1},{1,0},{2,3},{3,2},{4,5},{5,4},{6,7},{7,6},{8,9},{9,8},{10,11... | collective-permute-start | bytes 2359304 | tf_op jit(solution)/shard_map/ppermute | solution.py:100
  64.6 8.9 %collective-permute-done.5.refs_7_ = bf16[128,3072]{1,0:T(8,128)(2,1)S(1)} collective-permute-done((bf16[128,3072]{1,0:T(8,128)(2,1)}, bf16[128,3072]{1,0:T(8,128)(2,1)S(1)}, u32[]{:S(2)}, u32[]{:S(2)}) %collective-permute-start.5) | collective-permute-done | bytes 786464 | tf_op jit(solution)/shard_map/ppermute | solution.py:97
  73.5 7.7 %collective-permute-start.10 = (bf16[128,3072]{1,0:T(8,128)(2,1)S(1)}, bf16[128,3072]{1,0:T(8,128)(2,1)}, u32[]{:S(2)}, u32[]{:S(2)}) collective-permute-start(bf16[128,3072]{1,0:T(8,128)(2,1)S(1)} %collective-permute-done.2.refs_4_), channel_id=1, source_target_pairs={{0,1},{1,0},{2,3},{3,2},{4,5},{5,4},{6,7},{7,6},{8,9},{9,8},{10,11... | collective-permute-start | bytes 2359304 | tf_op jit(solution)/shard_map/ppermute | solution.py:100
  81.2 8.2 %collective-permute-done.6.refs_8_ = bf16[128,3072]{1,0:T(8,128)(2,1)} collective-permute-done((bf16[128,3072]{1,0:T(8,128)(2,1)}, bf16[128,3072]{1,0:T(8,128)(2,1)}, u32[]{:S(2)}, u32[]{:S(2)}) %collective-permute-start.6) | collective-permute-done | bytes 786464 | tf_op jit(solution)/shard_map/ppermute | solution.py:97
  89.4 5.6 %collective-permute-start.11 = (bf16[128,3072]{1,0:T(8,128)(2,1)S(1)}, bf16[128,3072]{1,0:T(8,128)(2,1)}, u32[]{:S(2)}, u32[]{:S(2)}) collective-permute-start(bf16[128,3072]{1,0:T(8,128)(2,1)S(1)} %collective-permute-done.3.refs_5_), channel_id=1, source_target_pairs={{0,1},{1,0},{2,3},{3,2},{4,5},{5,4},{6,7},{7,6},{8,9},{9,8},{10,11... | collective-permute-start | bytes 2359304 | tf_op jit(solution)/shard_map/ppermute | solution.py:100
  95.1 24.5 %all-gather = s32[16,1,128]{2,1,0:T(1,128)S(1)} all-gather(s32[1,1,128]{2,1,0:T(1,128)} %bitcast.37), channel_id=1, replica_groups=mesh['fsdp'=32,'tensor'=16] {'tensor'}, dimensions={0}, use_global_device_ids=true | all-gather | bytes 8704 | tf_op jit(solution)/shard_map/all_gather | solution.py:103
  121.5 2.1 %collective-permute-start.12 = (bf16[128,3072]{1,0:T(8,128)(2,1)S(1)}, bf16[128,3072]{1,0:T(8,128)(2,1)S(1)}, u32[]{:S(2)}, u32[]{:S(2)}) collective-permute-start(bf16[128,3072]{1,0:T(8,128)(2,1)S(1)} %collective-permute-done.4.refs_6_), channel_id=1, source_target_pairs={{0,1},{1,0},{2,3},{3,2},{4,5},{5,4},{6,7},{7,6},{8,9},{9,8},{10,11... | collective-permute-start | bytes 2359304 | tf_op jit(solution)/shard_map/ppermute | solution.py:100
  123.6 2.2 %collective-permute-start.13 = (bf16[128,3072]{1,0:T(8,128)(2,1)S(1)}, bf16[128,3072]{1,0:T(8,128)(2,1)S(1)}, u32[]{:S(2)}, u32[]{:S(2)}) collective-permute-start(bf16[128,3072]{1,0:T(8,128)(2,1)S(1)} %collective-permute-done.5.refs_7_), channel_id=1, source_target_pairs={{0,1},{1,0},{2,3},{3,2},{4,5},{5,4},{6,7},{7,6},{8,9},{9,8},{10,11... | collective-permute-start | bytes 2359304 | tf_op jit(solution)/shard_map/ppermute | solution.py:100
  125.9 2.1 %collective-permute-start.14 = (bf16[128,3072]{1,0:T(8,128)(2,1)}, bf16[128,3072]{1,0:T(8,128)(2,1)S(1)}, u32[]{:S(2)}, u32[]{:S(2)}) collective-permute-start(bf16[128,3072]{1,0:T(8,128)(2,1)} %collective-permute-done.6.refs_8_), channel_id=1, source_target_pairs={{0,1},{1,0},{2,3},{3,2},{4,5},{5,4},{6,7},{7,6},{8,9},{9,8},{10,11... | collective-permute-start | bytes 2359304 | tf_op jit(solution)/shard_map/ppermute | solution.py:100
  128.0 2.2 %collective-permute-start.8 = (bf16[128,3072]{1,0:T(8,128)(2,1)}, bf16[128,3072]{1,0:T(8,128)(2,1)S(1)}, u32[]{:S(2)}, u32[]{:S(2)}) collective-permute-start(bf16[128,3072]{1,0:T(8,128)(2,1)} %collective-permute-done.refs_2_), channel_id=1, source_target_pairs={{0,1},{1,0},{2,3},{3,2},{4,5},{5,4},{6,7},{7,6},{8,9},{9,8},{10,11... | collective-permute-start | bytes 2359304 | tf_op jit(solution)/shard_map/ppermute | solution.py:100
  130.2 2.1 %collective-permute-start.9 = (bf16[128,3072]{1,0:T(8,128)(2,1)}, bf16[128,3072]{1,0:T(8,128)(2,1)}, u32[]{:S(2)}, u32[]{:S(2)}) collective-permute-start(bf16[128,3072]{1,0:T(8,128)(2,1)} %collective-permute-done.1.refs_3_), channel_id=1, source_target_pairs={{0,1},{1,0},{2,3},{3,2},{4,5},{5,4},{6,7},{7,6},{8,9},{9,8},{10,11... | collective-permute-start | bytes 2359304 | tf_op jit(solution)/shard_map/ppermute | solution.py:100
  132.3 3.7 %fusion = (f32[2048,64]{1,0:T(8,128)S(1)}, f32[2048,64]{1,0:T(8,128)S(1)}, f32[2048,64]{1,0:T(8,128)S(1)}) fusion(f32[64]{0:T(128)S(1)} %multiply_power_fusion, f32[2048]{0:T(1024)S(1)} %bitcast.34), kind=kLoop, calls=%fused_computation.4 | loop fusion | flops 262144 | bytes 1581312 | tf_op jit(solution)/shard_map/neg | solution.py:64
  136.1 1.9 %pad_maximum_fusion = (f32[2048,128]{1,0:T(8,128)}, f32[2048,128]{1,0:T(8,128)}) fusion(f32[2048,64]{1,0:T(8,128)S(1)} %get-tuple-element.13, f32[2048,64]{1,0:T(8,128)S(1)} %get-tuple-element.12, f32[2048,64]{1,0:T(8,128)S(1)} %get-tuple-element.11), kind=kLoop, calls=%fused_computation.2 | loop fusion | flops 524288 | bytes 3670016 | tf_op jit(solution)/shard_map/concatenate | solution.py:64
  141.7 14.8 %shard_map.55 = bf16[3,2048,128]{2,1,0:T(8,128)(2,1)} custom-call(s32[16]{0:T(128)} %stack.67.refs_0_, bf16[128,3072]{1,0:T(8,128)(2,1)} %refs_1_, bf16[128,3072]{1,0:T(8,128)(2,1)} %collective-permute-done.refs_2_, bf16[128,3072]{1,0:T(8,128)(2,1)} %collective-permute-done.1.refs_3_, bf16[128,3072]{1,0:T(8,128)(2,1)} %copy-done, ...), custom_call_target="tpu_custom_call" | custom-call | flops 4831838208 | bytes 16515072 | tf_op jit(solution)/shard_map/pallas_call | solution.py:110
  (38 shorter events, 7.6 us)
Async XLA Ops:
  6.5 135.2 %all-gather.3.cloned.1.call-start = ((), (), s32[]{:S(2)}) async-start(), calls=%async_computation | async-start | bytes 2506752 | tf_op jit(solution)/shard_map/all_gather | solution.py:89
  6.5 5.9 %collective-permute-start.15 = (bf16[3,96,128]{2,1,0:T(8,128)(2,1)}, bf16[3,96,128]{2,1,0:T(8,128)(2,1)S(1)}, u32[]{:S(2)}, u32[]{:S(2)}) collective-permute-start(bf16[3,96,128]{2,1,0:T(8,128)(2,1)} %bitcast.33), channel_id=1, source_target_pairs={{0,16},{16,0},{32,48},{48,32},{64,80},{80,64},{96,112},{112,96},{1... | collective-permute-start | bytes 221192 | tf_op jit(solution)/shard_map/ppermute | solution.py:83
  14.0 20.6 %collective-permute-start.2 = (bf16[128,3072]{1,0:T(8,128)(2,1)}, bf16[128,3072]{1,0:T(8,128)(2,1)S(1)}, u32[]{:S(2)}, u32[]{:S(2)}) collective-permute-start(bf16[128,3072]{1,0:T(8,128)(2,1)} %refs_1_), channel_id=1, source_target_pairs={{0,8},{1,9},{2,10},{3,11},{4,12},{5,13},{6,14},{7,15},{8,0},{9,1},... | collective-permute-start | bytes 2359304 | tf_op jit(solution)/shard_map/ppermute | solution.py:97
  19.1 19.7 %collective-permute-start.3 = (bf16[128,3072]{1,0:T(8,128)(2,1)}, bf16[128,3072]{1,0:T(8,128)(2,1)S(1)}, u32[]{:S(2)}, u32[]{:S(2)}) collective-permute-start(bf16[128,3072]{1,0:T(8,128)(2,1)} %refs_1_), channel_id=1, source_target_pairs={{0,2},{1,3},{2,0},{3,1},{4,6},{5,7},{6,4},{7,5},{8,10},{9,11},{10,... | collective-permute-start | bytes 2359304 | tf_op jit(solution)/shard_map/ppermute | solution.py:97
  23.8 33.2 %collective-permute-start.4 = (bf16[128,3072]{1,0:T(8,128)(2,1)}, bf16[128,3072]{1,0:T(8,128)(2,1)S(1)}, u32[]{:S(2)}, u32[]{:S(2)}) collective-permute-start(bf16[128,3072]{1,0:T(8,128)(2,1)} %refs_1_), channel_id=1, source_target_pairs={{0,6},{1,7},{2,4},{3,5},{4,10},{5,11},{6,8},{7,9},{8,14},{9,15},{1... | collective-permute-start | bytes 2359304 | tf_op jit(solution)/shard_map/ppermute | solution.py:97
  26.0 47.5 %collective-permute-start.5 = (bf16[128,3072]{1,0:T(8,128)(2,1)}, bf16[128,3072]{1,0:T(8,128)(2,1)S(1)}, u32[]{:S(2)}, u32[]{:S(2)}) collective-permute-start(bf16[128,3072]{1,0:T(8,128)(2,1)} %refs_1_), channel_id=1, source_target_pairs={{0,14},{1,15},{2,12},{3,13},{4,2},{5,3},{6,0},{7,1},{8,6},{9,7},{1... | collective-permute-start | bytes 2359304 | tf_op jit(solution)/shard_map/ppermute | solution.py:97
  32.7 56.7 %collective-permute-start.6 = (bf16[128,3072]{1,0:T(8,128)(2,1)}, bf16[128,3072]{1,0:T(8,128)(2,1)}, u32[]{:S(2)}, u32[]{:S(2)}) collective-permute-start(bf16[128,3072]{1,0:T(8,128)(2,1)} %refs_1_), channel_id=1, source_target_pairs={{0,10},{1,11},{2,8},{3,9},{4,14},{5,15},{6,12},{7,13},{8,2},{9,3},... | collective-permute-start | bytes 2359304 | tf_op jit(solution)/shard_map/ppermute | solution.py:97
  34.6 103.4 %copy-start = (bf16[128,3072]{1,0:T(8,128)(2,1)}, bf16[128,3072]{1,0:T(8,128)(2,1)S(1)}, u32[]{:S(2)}) copy-start(bf16[128,3072]{1,0:T(8,128)(2,1)S(1)} %collective-permute-done.2.refs_4_) | copy-start | bytes 2359300
  34.6 86.9 %collective-permute-start = (bf16[128,3072]{1,0:T(8,128)(2,1)}, bf16[128,3072]{1,0:T(8,128)(2,1)}, u32[]{:S(2)}, u32[]{:S(2)}) collective-permute-start(bf16[128,3072]{1,0:T(8,128)(2,1)} %refs_1_), channel_id=1, source_target_pairs={{0,4},{1,5},{2,6},{3,7},{4,8},{5,9},{6,10},{7,11},{8,12},{9,13},{1... | collective-permute-start | bytes 2359304 | tf_op jit(solution)/shard_map/ppermute | solution.py:97
  38.8 99.2 %copy-start.1 = (bf16[128,3072]{1,0:T(8,128)(2,1)}, bf16[128,3072]{1,0:T(8,128)(2,1)S(1)}, u32[]{:S(2)}) copy-start(bf16[128,3072]{1,0:T(8,128)(2,1)S(1)} %collective-permute-done.3.refs_5_) | copy-start | bytes 2359300
  38.8 84.8 %collective-permute-start.1 = (bf16[128,3072]{1,0:T(8,128)(2,1)}, bf16[128,3072]{1,0:T(8,128)(2,1)}, u32[]{:S(2)}, u32[]{:S(2)}) collective-permute-start(bf16[128,3072]{1,0:T(8,128)(2,1)} %refs_1_), channel_id=1, source_target_pairs={{0,12},{1,13},{2,14},{3,15},{4,0},{5,1},{6,2},{7,3},{8,4},{9,5},{1... | collective-permute-start | bytes 2359304 | tf_op jit(solution)/shard_map/ppermute | solution.py:97
  57.0 81.0 %copy-start.2 = (bf16[128,3072]{1,0:T(8,128)(2,1)}, bf16[128,3072]{1,0:T(8,128)(2,1)S(1)}, u32[]{:S(2)}) copy-start(bf16[128,3072]{1,0:T(8,128)(2,1)S(1)} %collective-permute-done.4.refs_6_) | copy-start | bytes 2359300
  57.0 68.9 %collective-permute-start.7 = (bf16[128,3072]{1,0:T(8,128)(2,1)}, bf16[128,3072]{1,0:T(8,128)(2,1)}, u32[]{:S(2)}, u32[]{:S(2)}) collective-permute-start(bf16[128,3072]{1,0:T(8,128)(2,1)} %refs_1_), channel_id=1, source_target_pairs={{0,1},{1,0},{2,3},{3,2},{4,5},{5,4},{6,7},{7,6},{8,9},{9,8},{10,11... | collective-permute-start | bytes 2359304 | tf_op jit(solution)/shard_map/ppermute | solution.py:100
  73.5 64.5 %copy-start.3 = (bf16[128,3072]{1,0:T(8,128)(2,1)}, bf16[128,3072]{1,0:T(8,128)(2,1)S(1)}, u32[]{:S(2)}) copy-start(bf16[128,3072]{1,0:T(8,128)(2,1)S(1)} %collective-permute-done.5.refs_7_) | copy-start | bytes 2359300
  73.5 54.5 %collective-permute-start.10 = (bf16[128,3072]{1,0:T(8,128)(2,1)S(1)}, bf16[128,3072]{1,0:T(8,128)(2,1)}, u32[]{:S(2)}, u32[]{:S(2)}) collective-permute-start(bf16[128,3072]{1,0:T(8,128)(2,1)S(1)} %collective-permute-done.2.refs_4_), channel_id=1, source_target_pairs={{0,1},{1,0},{2,3},{3,2},{4,5},{5,4},{6,7},{7,6},{8,9},{9,8},{10,11... | collective-permute-start | bytes 2359304 | tf_op jit(solution)/shard_map/ppermute | solution.py:100
  89.4 40.8 %collective-permute-start.11 = (bf16[128,3072]{1,0:T(8,128)(2,1)S(1)}, bf16[128,3072]{1,0:T(8,128)(2,1)}, u32[]{:S(2)}, u32[]{:S(2)}) collective-permute-start(bf16[128,3072]{1,0:T(8,128)(2,1)S(1)} %collective-permute-done.3.refs_5_), channel_id=1, source_target_pairs={{0,1},{1,0},{2,3},{3,2},{4,5},{5,4},{6,7},{7,6},{8,9},{9,8},{10,11... | collective-permute-start | bytes 2359304 | tf_op jit(solution)/shard_map/ppermute | solution.py:100
  121.5 16.5 %collective-permute-start.12 = (bf16[128,3072]{1,0:T(8,128)(2,1)S(1)}, bf16[128,3072]{1,0:T(8,128)(2,1)S(1)}, u32[]{:S(2)}, u32[]{:S(2)}) collective-permute-start(bf16[128,3072]{1,0:T(8,128)(2,1)S(1)} %collective-permute-done.4.refs_6_), channel_id=1, source_target_pairs={{0,1},{1,0},{2,3},{3,2},{4,5},{5,4},{6,7},{7,6},{8,9},{9,8},{10,11... | collective-permute-start | bytes 2359304 | tf_op jit(solution)/shard_map/ppermute | solution.py:100
  123.6 14.4 %collective-permute-start.13 = (bf16[128,3072]{1,0:T(8,128)(2,1)S(1)}, bf16[128,3072]{1,0:T(8,128)(2,1)S(1)}, u32[]{:S(2)}, u32[]{:S(2)}) collective-permute-start(bf16[128,3072]{1,0:T(8,128)(2,1)S(1)} %collective-permute-done.5.refs_7_), channel_id=1, source_target_pairs={{0,1},{1,0},{2,3},{3,2},{4,5},{5,4},{6,7},{7,6},{8,9},{9,8},{10,11... | collective-permute-start | bytes 2359304 | tf_op jit(solution)/shard_map/ppermute | solution.py:100
  125.9 13.1 %collective-permute-start.14 = (bf16[128,3072]{1,0:T(8,128)(2,1)}, bf16[128,3072]{1,0:T(8,128)(2,1)S(1)}, u32[]{:S(2)}, u32[]{:S(2)}) collective-permute-start(bf16[128,3072]{1,0:T(8,128)(2,1)} %collective-permute-done.6.refs_8_), channel_id=1, source_target_pairs={{0,1},{1,0},{2,3},{3,2},{4,5},{5,4},{6,7},{7,6},{8,9},{9,8},{10,11... | collective-permute-start | bytes 2359304 | tf_op jit(solution)/shard_map/ppermute | solution.py:100
  128.0 11.8 %collective-permute-start.8 = (bf16[128,3072]{1,0:T(8,128)(2,1)}, bf16[128,3072]{1,0:T(8,128)(2,1)S(1)}, u32[]{:S(2)}, u32[]{:S(2)}) collective-permute-start(bf16[128,3072]{1,0:T(8,128)(2,1)} %collective-permute-done.refs_2_), channel_id=1, source_target_pairs={{0,1},{1,0},{2,3},{3,2},{4,5},{5,4},{6,7},{7,6},{8,9},{9,8},{10,11... | collective-permute-start | bytes 2359304 | tf_op jit(solution)/shard_map/ppermute | solution.py:100
  130.2 11.5 %collective-permute-start.9 = (bf16[128,3072]{1,0:T(8,128)(2,1)}, bf16[128,3072]{1,0:T(8,128)(2,1)}, u32[]{:S(2)}, u32[]{:S(2)}) collective-permute-start(bf16[128,3072]{1,0:T(8,128)(2,1)} %collective-permute-done.1.refs_3_), channel_id=1, source_target_pairs={{0,1},{1,0},{2,3},{3,2},{4,5},{5,4},{6,7},{7,6},{8,9},{9,8},{10,11... | collective-permute-start | bytes 2359304 | tf_op jit(solution)/shard_map/ppermute | solution.py:100
  138.9 0.9 copy-start.5
  139.8 0.9 copy-start.6
  140.8 0.9 copy-start.7
  (1 other events, 0.9 us)
Sparse Core Ops, SparseCore 0:
  14.1 72.3 all-gather.2

commit v2 on v0

v2 whole, which is shorter than its diff:
```python
import jax
import jax.numpy as jnp
from jax import lax
from jax.experimental import pallas as pl
from jax.experimental.pallas import tpu as pltpu
from jax.sharding import Mesh
from jax.sharding import PartitionSpec as P

HEAD_DIM = 128
SEQ_LEN = 1024
rope_base = 10000.0

Y, X_HI, CORE = 4, 2, 2
BATCH = 4
NEAR = 64


def keys_kernel(where_ref, *refs):
    count = Y + 2
    (*near_own, far_own_ref, far_other_ref), (*near_across, x_far_own_ref, x_far_other_ref) = refs[:count], refs[count : 2 * count]
    refs = refs[2 * count :]
    w_ref, bias_ref, taps_ref, turns_ref, out_ref, held, w_flat, turns, keys, turns_sem, out_sems, w_sems, sems = refs
    shards, rows, depth = held.shape
    pieces, heads = w_ref.shape[0], out_ref.shape[0]
    piece_rows = w_ref.shape[1] // heads
    my_x, my_core, my_y = where_ref[0], where_ref[1], where_ref[2]
    loads = []
    for piece in range(pieces):
        for head in range(heads):
            loads.append(
                pltpu.make_async_copy(
                    w_ref.at[piece, pl.ds(head * piece_rows, piece_rows), :],
                    w_flat.at[pl.ds(piece * piece_rows, piece_rows), pl.ds(head * HEAD_DIM, HEAD_DIM)],
                    w_sems.at[piece * heads + head],
                )
            )
    per_block = BATCH // (X_HI * CORE)

    def copies_of(y, source_y, kept):
        copies = []
        for x_step in range(X_HI):
            chip = y * X_HI + jnp.bitwise_xor(my_x, x_step)
            for core_step, near, far in (
                (0, near_own[kept], (far_own_ref, far_other_ref)[x_step]),
                (1, near_across[kept], (x_far_own_ref, x_far_other_ref)[x_step]),
            ):
                shard = chip * CORE + jnp.bitwise_xor(my_core, core_step)
                for source, start, size in ((near.at[x_step], 0, NEAR), (far.at[source_y], NEAR, rows - NEAR)):
                    number = y * 2 * X_HI * CORE + len(copies)
                    copies.append(pltpu.make_async_copy(source, held.at[shard, pl.ds(start, size), :], sems.at[number]))
        return copies

    def start_block(block):
        for y in range(block * per_block, (block + 1) * per_block):
            source_y = lax.rem(my_y - y + Y, Y)
            for kept in range(Y):

                @pl.when(source_y == kept)
                def _():
                    for copy in copies_of(y, kept, kept):
                        copy.start()

    def wait_block(block):
        for y in range(block * per_block, (block + 1) * per_block):
            for copy in copies_of(y, 0, 0):
                copy.wait()

    load_turns = pltpu.make_async_copy(turns_ref, turns, turns_sem)
    for load in loads:
        load.start()
    start_block(0)
    load_turns.start()
    for load in loads:
        load.wait()

    block_rows = BATCH * rows
    row = lax.broadcasted_iota(jnp.int32, (block_rows, HEAD_DIM), 0)
    is_first = lax.broadcasted_iota(jnp.int32, (block_rows, HEAD_DIM), 1) < HEAD_DIM // 2
    stores = []
    tail = None
    for first in range(0, shards, BATCH):
        if first + BATCH < shards:
            start_block(first // BATCH + 1)
        wait_block(first // BATCH)
        start = first * rows
        block = held[first : first + BATCH].reshape(block_rows, depth)
        projected = jnp.dot(block, w_flat[...], preferred_element_type=jnp.float32) + bias_ref[...]
        if start % SEQ_LEN == 0:
            tail = jnp.zeros((8, projected.shape[1]), jnp.float32)
        if first == 0:
            load_turns.wait()
        turn = turns[start : start + block_rows, :]
        other_turn = pltpu.roll(turn, HEAD_DIM // 2, 1)
        cosine = jnp.where(is_first, turn, other_turn)
        sine = jnp.where(is_first, -other_turn, turn)
        for head in range(heads):
            lanes = slice(head * HEAD_DIM, (head + 1) * HEAD_DIM)
            now = projected[:, lanes]
            before_one, before_two = tail[7:8, lanes], tail[6:7, lanes]
            previous_one = jnp.where(row == 0, before_one, pltpu.roll(now, 1, 0))
            previous_two = jnp.where(row == 0, before_two, jnp.where(row == 1, before_one, pltpu.roll(now, 2, 0)))
            part = taps_ref[0:1, lanes] * now + taps_ref[1:2, lanes] * previous_one + taps_ref[2:3, lanes] * previous_two
            turned = part * cosine + pltpu.roll(part, HEAD_DIM // 2, 1) * sine
            keys[head, start : start + block_rows, :] = turned.astype(keys.dtype)
        tail = projected[block_rows - 8 :]
        span = pl.ds(start, block_rows)
        stores.append(pltpu.make_async_copy(keys.at[:, span, :], out_ref.at[:, span, :], out_sems.at[first // BATCH]))
        stores[-1].start()
    for store in stores:
        store.wait()


def gate_kernel(*refs):
    del refs


def gated(value, *after):
    any_space = pl.BlockSpec(memory_space=pl.ANY)
    return pl.pallas_call(
        gate_kernel,
        in_specs=[any_space] * (1 + len(after)),
        out_specs=any_space,
        out_shape=jax.ShapeDtypeStruct(value.shape, value.dtype),
        input_output_aliases={0: 0},
        compiler_params=pltpu.CompilerParams(vmem_limit_bytes=2 * 1024 * 1024),
    )(value, *after)


def rotation(places):
    half_dim = HEAD_DIM // 2
    inv_freq = rope_base ** (-(jnp.arange(half_dim, dtype=jnp.float32) * 2.0) / HEAD_DIM)
    angles = places.astype(jnp.float32)[:, None] * inv_freq[None, :]
    return jnp.concatenate([jnp.cos(angles), jnp.sin(angles)], axis=1)


def keys_of(where, gathered, weight, bias, taps, turns):
    rows, depth = gathered[0].shape[1] + gathered[Y].shape[1], gathered[0].shape[2]
    shards = Y * X_HI * CORE
    columns = bias.shape[1]
    heads = columns // HEAD_DIM
    total = shards * rows
    vmem, any_space = pl.BlockSpec(memory_space=pltpu.VMEM), pl.BlockSpec(memory_space=pl.ANY)
    return pl.pallas_call(
        keys_kernel,
        in_specs=[pl.BlockSpec(memory_space=pltpu.SMEM)] + [any_space] * (len(gathered) + 1) + [vmem] * 2 + [any_space],
        out_specs=any_space,
        out_shape=jax.ShapeDtypeStruct((heads, total, HEAD_DIM), jnp.bfloat16),
        scratch_shapes=[
            pltpu.VMEM((shards, rows, depth), jnp.bfloat16),
            pltpu.VMEM((depth, columns), jnp.bfloat16),
            pltpu.VMEM((total, HEAD_DIM), jnp.float32),
            pltpu.VMEM((heads, total, HEAD_DIM), jnp.bfloat16),
            pltpu.SemaphoreType.DMA,
            pltpu.SemaphoreType.DMA((shards // BATCH,)),
            pltpu.SemaphoreType.DMA((weight.shape[0] * heads,)),
            pltpu.SemaphoreType.DMA((2 * shards,)),
        ],
        compiler_params=pltpu.CompilerParams(vmem_limit_bytes=56 * 1024 * 1024),
        cost_estimate=pl.CostEstimate(
            flops=2 * total * depth * columns,
            bytes_accessed=2 * (total * depth + depth * columns + total * columns),
            transcendentals=0,
        ),
    )(where, *gathered, weight, bias, taps, turns)


def along_y(value):
    def step(k):
        return lax.ppermute(value, "y", [(i, (i + k) % Y) for i in range(Y)])

    return [value] + [step(k) for k in range(1, Y)]


def body(fsdp, tensor, tokens, positions, key_weight, key_bias, conv_taps):
    rows, depth = tokens.shape
    piece, heads, _ = key_weight.shape
    columns = heads * HEAD_DIM

    own_weight = jnp.transpose(key_weight, (1, 0, 2))
    near_weight = lax.ppermute(own_weight, "x_lo", [(0, 1), (1, 0)])
    is_low = lax.axis_index("x_lo") == 0
    first = jnp.where(is_low, own_weight, near_weight)
    second = jnp.where(is_low, near_weight, own_weight)
    pair = jnp.concatenate([first, second], axis=1).reshape(heads * 2 * piece, HEAD_DIM)
    weight = lax.all_gather(pair, "z", axis=0)

    across = [(0, 1), (1, 0)]
    near, far = gated(tokens[:NEAR], pair), gated(tokens[NEAR:], pair)
    x_near = lax.ppermute(near, "x_hi", across)
    sent = jnp.broadcast_to(positions[None], (tensor, rows))
    places = lax.all_to_all(sent, ("y", "x_hi", "core"), 0, 0, tiled=True).reshape(-1)
    far_own = gated(jnp.stack(along_y(far)), x_near, places)
    far_other = lax.ppermute(far_own, "x_hi", across)
    near_all = along_y(gated(jnp.stack([near, x_near]), far_own))
    turns = rotation(gated(places, near_all[1]))
    near_all[2:] = [gated(piece, turns) for piece in near_all[2:]]
    gathered = (*near_all, far_own, far_other)
    gathered += tuple(lax.ppermute(piece, "core", across) for piece in gathered)
    where = jnp.stack([lax.axis_index("x_hi"), lax.axis_index("core"), lax.axis_index("y")])

    taps = jnp.transpose(conv_taps, (1, 0, 2)).reshape(conv_taps.shape[1], columns)
    bias = key_bias.astype(jnp.float32).reshape(1, columns)
    keys = keys_of(where, gathered, weight, bias, taps, turns)
    return jnp.transpose(keys, (1, 0, 2))


def solution(mesh):
    fsdp, tensor = mesh.shape["fsdp"], mesh.shape["tensor"]
    split = Mesh(mesh.devices.reshape(fsdp // 2, 2, Y, X_HI, CORE), ("z", "x_lo", "y", "x_hi", "core"))
    rows, heads = ("z", "x_lo"), ("y", "x_hi", "core")
    return jax.shard_map(
        lambda *args: body(fsdp, tensor, *args),
        mesh=split,
        in_specs=(P(rows + heads, None), P(rows + heads), P(rows, heads, None), P(heads, None), P(heads, None, None)),
        out_specs=P(rows, heads, None),
        check_vma=False,
    )
```

time: 280 us -> 130 us (0.46)
  waiting for transfers between devices: 216 us -> 18.7 us
  starting transfers between devices: 0.04 us -> 71.3 us
  blocking collectives: 25.8 us -> 0 us
  Pallas kernels: 0 us -> 13.5 us
  matrix products: 10.5 us -> 0 us
    all_gather x2 -> x1, waiting for transfers between devices: 215 us -> 0.01 us  [body(): weight = lax.all_gather(pair, 'z', axis=0)]
    ppermute x0 -> x15, starting transfers between devices: none -> 60.2 us  [the longest x6 31 us: body(): lax.ppermute(piece, 'core', across)]
    all_gather x1 -> x0, blocking collectives: 25.8 us -> none  [body(): lax.all_gather(positions, 'tensor', axis=0, tiled=True)]
    ppermute x0 -> x15, waiting for transfers between devices: none -> 13.7 us  [the longest x6 11.2 us: step(): return lax.ppermute(value, 'y', [(i, (i + k) % Y) for i in range(Y)])]
    pallas_call x0 -> x8, Pallas kernels: none -> 13.5 us  [the longest x1 13.5 us: keys_of(): pl.pallas_call(keys_kernel, in_specs=[pl.BlockSpec(memory_space=pltpu.SME...]
    all_to_all x0 -> x1, starting transfers between devices: none -> 11.1 us  [body(): lax.all_to_all(sent, ('y', 'x_hi', 'core'), 0, 0, tiled=True).reshape(-1)]
    dot_general x1 -> x0, matrix products: 10.5 us -> none  [body(): jnp.dot(seq_tokens, weight_piece.reshape(piece_rows, columns), preferred_...]
    all_to_all x0 -> x1, waiting for transfers between devices: none -> 5.02 us  [body(): lax.all_to_all(sent, ('y', 'x_hi', 'core'), 0, 0, tiled=True).reshape(-1)]
  transfers between devices with their start and end apart: 2 -> 17, of which waited for: 2 -> 4; matrix products, arithmetic and copies ran while one was open for 3% -> 6% of each run, Pallas kernels for 0% -> 0%
where the time goes in v2:
time: 130 us; the launch traced here: 129 us
  starting transfers between devices  71.3 us (55%)
  waiting for transfers between devices  18.7 us (14%)
  between operations  13.8 us (11%)
  Pallas kernels  13.5 us (10%)
  other arithmetic  7.51 us (6%)
  local copies, waits for them, and re-layouts  4.15 us (3%)
    ppermute x6, starting transfers between devices, body(): lax.ppermute(piece, 'core', across)  31 us
    ppermute x6, starting transfers between devices, step(): return lax.ppermute(value, 'y', [(i, (i + k) % Y) for i in range(Y)])  18.3 us
    pallas_call x1, Pallas kernels, keys_of(): pl.pallas_call(keys_kernel, in_specs=[pl.BlockSpec(memory_space=pltpu.SME...  13.5 us
    ppermute x6, waiting for transfers between devices, step(): return lax.ppermute(value, 'y', [(i, (i + k) % Y) for i in range(Y)])  11.2 us
    all_to_all x1, starting transfers between devices, body(): lax.all_to_all(sent, ('y', 'x_hi', 'core'), 0, 0, tiled=True).reshape(-1)  11.1 us
    all_to_all x1, waiting for transfers between devices, body(): lax.all_to_all(sent, ('y', 'x_hi', 'core'), 0, 0, tiled=True).reshape(-1)  5.02 us
    ppermute x1, starting transfers between devices, body(): x_near = lax.ppermute(near, 'x_hi', across)  4.65 us
    ppermute x1, starting transfers between devices, body(): near_weight = lax.ppermute(own_weight, 'x_lo', [(0, 1), (1, 0)])  3.94 us
  transfers between devices with their start and end apart: 17, of which 4 were waited for; matrix products, arithmetic and copies ran while one was open for 6% of the time, Pallas kernels for 0%

profile of v2, /device:TPU:1, one launch (start us, length us, event | category | flops | bytes accessed | tf_op | source)
XLA Modules:
  0.0 129.0 jit_solution(2810258072339827716)
XLA Ops:
  6.5 3.9 %collective-permute-start = (bf16[3,96,128]{2,1,0:T(8,128)(2,1)}, bf16[3,96,128]{2,1,0:T(8,128)(2,1)S(1)}, u32[]{:S(2)}, u32[]{:S(2)}) collective-permute-start(bf16[3,96,128]{2,1,0:T(8,128)(2,1)} %bitcast.36), channel_id=1, source_target_pairs={{0,16},{16,0},{1,17},{17,1},{2,18},{18,2},{3,19},{19,3},{4,20},{20... | collective-permute-start | bytes 221192 | tf_op jit(solution)/shard_map/ppermute | solution.py:180
  10.5 1.9 %collective-permute-done = bf16[3,96,128]{2,1,0:T(8,128)(2,1)S(1)} collective-permute-done((bf16[3,96,128]{2,1,0:T(8,128)(2,1)}, bf16[3,96,128]{2,1,0:T(8,128)(2,1)S(1)}, u32[]{:S(2)}, u32[]{:S(2)}) %collective-permute-start) | collective-permute-done | bytes 73760 | tf_op jit(solution)/shard_map/ppermute | solution.py:180
  14.0 1.2 fusion
  15.3 4.9 %collective-permute-start.4 = (bf16[64,3072]{1,0:T(8,128)(2,1)S(1)}, bf16[64,3072]{1,0:T(8,128)(2,1)S(1)}, u32[]{:S(2)}, u32[]{:S(2)}) collective-permute-start(bf16[64,3072]{1,0:T(8,128)(2,1)S(1)} %shard_map.56), channel_id=1, source_target_pairs={{0,12},{4,0},{8,4},{12,8},{1,13},{5,1},{9,5},{13,9},{2,14},{6,2},{... | collective-permute-start | bytes 1179656 | tf_op jit(solution)/shard_map/ppermute | solution.py:169
  20.1 2.3 %collective-permute-start.3 = (bf16[64,3072]{1,0:T(8,128)(2,1)S(1)}, bf16[64,3072]{1,0:T(8,128)(2,1)S(1)}, u32[]{:S(2)}, u32[]{:S(2)}) collective-permute-start(bf16[64,3072]{1,0:T(8,128)(2,1)S(1)} %shard_map.56), channel_id=1, source_target_pairs={{0,8},{4,12},{8,0},{12,4},{1,9},{5,13},{9,1},{13,5},{2,10},{6,14},... | collective-permute-start | bytes 1179656 | tf_op jit(solution)/shard_map/ppermute | solution.py:169
  22.4 2.6 %collective-permute-start.2 = (bf16[64,3072]{1,0:T(8,128)(2,1)S(1)}, bf16[64,3072]{1,0:T(8,128)(2,1)S(1)}, u32[]{:S(2)}, u32[]{:S(2)}) collective-permute-start(bf16[64,3072]{1,0:T(8,128)(2,1)S(1)} %shard_map.56), channel_id=1, source_target_pairs={{0,4},{4,8},{8,12},{12,0},{1,5},{5,9},{9,13},{13,1},{2,6},{6,10},{... | collective-permute-start | bytes 1179656 | tf_op jit(solution)/shard_map/ppermute | solution.py:169
  25.0 4.7 %collective-permute-start.1 = (bf16[64,3072]{1,0:T(8,128)(2,1)S(1)}, bf16[64,3072]{1,0:T(8,128)(2,1)S(1)}, u32[]{:S(2)}, u32[]{:S(2)}) collective-permute-start(bf16[64,3072]{1,0:T(8,128)(2,1)S(1)} %shard_map.55), channel_id=1, source_target_pairs={{0,2},{2,0},{1,3},{3,1},{4,6},{6,4},{5,7},{7,5},{8,10},{10,8},{9,1... | collective-permute-start | bytes 1179656 | tf_op jit(solution)/shard_map/ppermute | solution.py:189
  30.3 11.1 %all-to-all-start = ((s32[16,1,128]{2,1,0:T(1,128)}), s32[16,1,128]{2,1,0:T(1,128)S(1)}, u32[]{:S(2)}, u32[]{:S(2)}) async-start(s32[16,1,128]{2,1,0:T(1,128)} %broadcast_in_dim.2), calls=%async_computation | async-start | bytes 16384 | tf_op jit(solution)/shard_map/all_to_all | solution.py:191
  42.2 1.2 pad_maximum_fusion.refs_0_
  43.4 5.0 %all-to-all-done = s32[16,1,128]{2,1,0:T(1,128)S(1)} async-done(((s32[16,1,128]{2,1,0:T(1,128)}), s32[16,1,128]{2,1,0:T(1,128)S(1)}, u32[]{:S(2)}, u32[]{:S(2)}) %all-to-all-start) | async-done | bytes 8224 | tf_op jit(solution)/shard_map/all_to_all | solution.py:191
  48.4 2.3 %collective-permute-start.8 = (bf16[4,64,3072]{2,1,0:T(8,128)(2,1)S(1)}, bf16[4,64,3072]{2,1,0:T(8,128)(2,1)}, u32[]{:S(2)}, u32[]{:S(2)}) collective-permute-start(bf16[4,64,3072]{2,1,0:T(8,128)(2,1)S(1)} %shard_map.57.refs_1_.refs_4_), channel_id=1, source_target_pairs={{0,2},{2,0},{1,3},{3,1},{4,6},{6,4},{5,7},{7,5},{8,10},{10,8},{9,1... | collective-permute-start | bytes 4718600 | tf_op jit(solution)/shard_map/ppermute | solution.py:193
  50.8 2.5 %collective-permute-start.5 = (bf16[2,64,3072]{2,1,0:T(8,128)(2,1)S(1)}, bf16[2,64,3072]{2,1,0:T(8,128)(2,1)S(1)}, u32[]{:S(2)}, u32[]{:S(2)}) collective-permute-start(bf16[2,64,3072]{2,1,0:T(8,128)(2,1)S(1)} %shard_map.58.refs_0_), channel_id=1, source_target_pairs={{0,4},{4,8},{8,12},{12,0},{1,5},{5,9},{9,13},{13,1},{2,6},{6,10},{... | collective-permute-start | bytes 2359304 | tf_op jit(solution)/shard_map/ppermute | solution.py:169
  53.3 2.7 %collective-permute-start.9 = (bf16[2,64,3072]{2,1,0:T(8,128)(2,1)S(1)}, bf16[2,64,3072]{2,1,0:T(8,128)(2,1)S(1)}, u32[]{:S(2)}, u32[]{:S(2)}) collective-permute-start(bf16[2,64,3072]{2,1,0:T(8,128)(2,1)S(1)} %shard_map.58.refs_0_), channel_id=1, source_target_pairs={{0,1},{1,0},{2,3},{3,2},{4,5},{5,4},{6,7},{7,6},{8,9},{9,8},{10,11... | collective-permute-start | bytes 2359304 | tf_op jit(solution)/shard_map/ppermute | solution.py:198
  56.0 4.2 %collective-permute-start.7 = (bf16[2,64,3072]{2,1,0:T(8,128)(2,1)S(1)}, bf16[2,64,3072]{2,1,0:T(8,128)(2,1)S(1)}, u32[]{:S(2)}, u32[]{:S(2)}) collective-permute-start(bf16[2,64,3072]{2,1,0:T(8,128)(2,1)S(1)} %shard_map.58.refs_0_), channel_id=1, source_target_pairs={{0,12},{4,0},{8,4},{12,8},{1,13},{5,1},{9,5},{13,9},{2,14},{6,2},{... | collective-permute-start | bytes 2359304 | tf_op jit(solution)/shard_map/ppermute | solution.py:169
  60.2 1.9 %collective-permute-start.6 = (bf16[2,64,3072]{2,1,0:T(8,128)(2,1)S(1)}, bf16[2,64,3072]{2,1,0:T(8,128)(2,1)}, u32[]{:S(2)}, u32[]{:S(2)}) collective-permute-start(bf16[2,64,3072]{2,1,0:T(8,128)(2,1)S(1)} %shard_map.58.refs_0_), channel_id=1, source_target_pairs={{0,8},{4,12},{8,0},{12,4},{1,9},{5,13},{9,1},{13,5},{2,10},{6,14},... | collective-permute-start | bytes 2359304 | tf_op jit(solution)/shard_map/ppermute | solution.py:169
  62.1 11.2 %collective-permute-done.5.refs_1_ = bf16[2,64,3072]{2,1,0:T(8,128)(2,1)S(1)} collective-permute-done((bf16[2,64,3072]{2,1,0:T(8,128)(2,1)S(1)}, bf16[2,64,3072]{2,1,0:T(8,128)(2,1)S(1)}, u32[]{:S(2)}, u32[]{:S(2)}) %collective-permute-start.5) | collective-permute-done | bytes 786464 | tf_op jit(solution)/shard_map/ppermute | solution.py:169
  73.3 19.3 %collective-permute-start.13 = (bf16[4,64,3072]{2,1,0:T(8,128)(2,1)S(1)}, bf16[4,64,3072]{2,1,0:T(8,128)(2,1)}, u32[]{:S(2)}, u32[]{:S(2)}) collective-permute-start(bf16[4,64,3072]{2,1,0:T(8,128)(2,1)S(1)} %shard_map.57.refs_1_.refs_4_), channel_id=1, source_target_pairs={{0,1},{1,0},{2,3},{3,2},{4,5},{5,4},{6,7},{7,6},{8,9},{9,8},{10,11... | collective-permute-start | bytes 4718600 | tf_op jit(solution)/shard_map/ppermute | solution.py:198
  92.6 1.9 %collective-permute-start.14 = (bf16[4,64,3072]{2,1,0:T(8,128)(2,1)}, bf16[4,64,3072]{2,1,0:T(8,128)(2,1)}, u32[]{:S(2)}, u32[]{:S(2)}) collective-permute-start(bf16[4,64,3072]{2,1,0:T(8,128)(2,1)} %collective-permute-done.8.refs_5_), channel_id=1, source_target_pairs={{0,1},{1,0},{2,3},{3,2},{4,5},{5,4},{6,7},{7,6},{8,9},{9,8},{10,11... | collective-permute-start | bytes 4718600 | tf_op jit(solution)/shard_map/ppermute | solution.py:198
  94.6 3.7 %multiply_cosine_fusion = (f32[2048,64]{1,0:T(8,128)S(1)}, f32[2048,64]{1,0:T(8,128)S(1)}) fusion(f32[64]{0:T(128)S(1)} %multiply_power_fusion, f32[2048]{0:T(1024)S(1)} %convert_element_type.4), kind=kLoop, calls=%fused_computation.2 | loop fusion | flops 131072 | bytes 1057024 | tf_op jit(solution)/shard_map/cos | solution.py:133
  98.7 2.5 %collective-permute-start.11 = (bf16[2,64,3072]{2,1,0:T(8,128)(2,1)}, bf16[2,64,3072]{2,1,0:T(8,128)(2,1)}, u32[]{:S(2)}, u32[]{:S(2)}) collective-permute-start(bf16[2,64,3072]{2,1,0:T(8,128)(2,1)} %shard_map.60.refs_2_), channel_id=1, source_target_pairs={{0,1},{1,0},{2,3},{3,2},{4,5},{5,4},{6,7},{7,6},{8,9},{9,8},{10,11... | collective-permute-start | bytes 2359304 | tf_op jit(solution)/shard_map/ppermute | solution.py:198
  101.2 1.9 %collective-permute-start.10 = (bf16[2,64,3072]{2,1,0:T(8,128)(2,1)S(1)}, bf16[2,64,3072]{2,1,0:T(8,128)(2,1)}, u32[]{:S(2)}, u32[]{:S(2)}) collective-permute-start(bf16[2,64,3072]{2,1,0:T(8,128)(2,1)S(1)} %collective-permute-done.5.refs_1_), channel_id=1, source_target_pairs={{0,1},{1,0},{2,3},{3,2},{4,5},{5,4},{6,7},{7,6},{8,9},{9,8},{10,11... | collective-permute-start | bytes 2359304 | tf_op jit(solution)/shard_map/ppermute | solution.py:198
  103.2 1.0 copy-done.9
  104.2 2.6 %collective-permute-start.12 = (bf16[2,64,3072]{2,1,0:T(8,128)(2,1)S(1)}, bf16[2,64,3072]{2,1,0:T(8,128)(2,1)}, u32[]{:S(2)}, u32[]{:S(2)}) collective-permute-start(bf16[2,64,3072]{2,1,0:T(8,128)(2,1)S(1)} %shard_map.61.refs_3_), channel_id=1, source_target_pairs={{0,1},{1,0},{2,3},{3,2},{4,5},{5,4},{6,7},{7,6},{8,9},{9,8},{10,11... | collective-permute-start | bytes 2359304 | tf_op jit(solution)/shard_map/ppermute | solution.py:198
  108.6 13.5 %shard_map.62 = bf16[3,2048,128]{2,1,0:T(8,128)(2,1)} custom-call(s32[3]{0:T(128)} %pad_add_fusion.where_ref, bf16[2,64,3072]{2,1,0:T(8,128)(2,1)} %copy-done.2, bf16[2,64,3072]{2,1,0:T(8,128)(2,1)} %copy-done.4, bf16[2,64,3072]{2,1,0:T(8,128)(2,1)} %shard_map.60.refs_2_, bf16[2,64,3072]{2,1,0:T(8,128)(2,1)} %copy-done.5, bf16[4,64,3072]{2,1,0:T(8,128)(2,1)} %copy-done, ...), custom_call_target="tpu_custom_call" | custom-call | flops 4831838208 | bytes 16515072 | tf_op jit(solution)/shard_map/pallas_call | solution.py:143
  (52 shorter events, 5.2 us)
Async XLA Ops:
  6.5 102.1 %all-gather.2.cloned.1.call-start = ((), (), s32[]{:S(2)}) async-start(), calls=%async_computation.1 | async-start | bytes 2506752 | tf_op jit(solution)/shard_map/all_gather | solution.py:185
  6.5 5.9 %collective-permute-start = (bf16[3,96,128]{2,1,0:T(8,128)(2,1)}, bf16[3,96,128]{2,1,0:T(8,128)(2,1)S(1)}, u32[]{:S(2)}, u32[]{:S(2)}) collective-permute-start(bf16[3,96,128]{2,1,0:T(8,128)(2,1)} %bitcast.36), channel_id=1, source_target_pairs={{0,16},{16,0},{1,17},{17,1},{2,18},{18,2},{3,19},{19,3},{4,20},{20... | collective-permute-start | bytes 221192 | tf_op jit(solution)/shard_map/ppermute | solution.py:180
  14.0 15.7 %copy-start.8 = (s32[128]{0:T(128)S(1)}, s32[128]{0:T(128)}, u32[]{:S(2)}) copy-start(s32[128]{0:T(128)} %param.6) | copy-start | bytes 1540
  15.3 26.1 %collective-permute-start.4 = (bf16[64,3072]{1,0:T(8,128)(2,1)S(1)}, bf16[64,3072]{1,0:T(8,128)(2,1)S(1)}, u32[]{:S(2)}, u32[]{:S(2)}) collective-permute-start(bf16[64,3072]{1,0:T(8,128)(2,1)S(1)} %shard_map.56), channel_id=1, source_target_pairs={{0,12},{4,0},{8,4},{12,8},{1,13},{5,1},{9,5},{13,9},{2,14},{6,2},{... | collective-permute-start | bytes 1179656 | tf_op jit(solution)/shard_map/ppermute | solution.py:169
  20.1 21.3 %collective-permute-start.3 = (bf16[64,3072]{1,0:T(8,128)(2,1)S(1)}, bf16[64,3072]{1,0:T(8,128)(2,1)S(1)}, u32[]{:S(2)}, u32[]{:S(2)}) collective-permute-start(bf16[64,3072]{1,0:T(8,128)(2,1)S(1)} %shard_map.56), channel_id=1, source_target_pairs={{0,8},{4,12},{8,0},{12,4},{1,9},{5,13},{9,1},{13,5},{2,10},{6,14},... | collective-permute-start | bytes 1179656 | tf_op jit(solution)/shard_map/ppermute | solution.py:169
  22.4 19.0 %collective-permute-start.2 = (bf16[64,3072]{1,0:T(8,128)(2,1)S(1)}, bf16[64,3072]{1,0:T(8,128)(2,1)S(1)}, u32[]{:S(2)}, u32[]{:S(2)}) collective-permute-start(bf16[64,3072]{1,0:T(8,128)(2,1)S(1)} %shard_map.56), channel_id=1, source_target_pairs={{0,4},{4,8},{8,12},{12,0},{1,5},{5,9},{9,13},{13,1},{2,6},{6,10},{... | collective-permute-start | bytes 1179656 | tf_op jit(solution)/shard_map/ppermute | solution.py:169
  25.0 23.4 %collective-permute-start.1 = (bf16[64,3072]{1,0:T(8,128)(2,1)S(1)}, bf16[64,3072]{1,0:T(8,128)(2,1)S(1)}, u32[]{:S(2)}, u32[]{:S(2)}) collective-permute-start(bf16[64,3072]{1,0:T(8,128)(2,1)S(1)} %shard_map.55), channel_id=1, source_target_pairs={{0,2},{2,0},{1,3},{3,1},{4,6},{6,4},{5,7},{7,5},{8,10},{10,8},{9,1... | collective-permute-start | bytes 1179656 | tf_op jit(solution)/shard_map/ppermute | solution.py:189
  30.3 18.1 %all-to-all-start = ((s32[16,1,128]{2,1,0:T(1,128)}), s32[16,1,128]{2,1,0:T(1,128)S(1)}, u32[]{:S(2)}, u32[]{:S(2)}) async-start(s32[16,1,128]{2,1,0:T(1,128)} %broadcast_in_dim.2), calls=%async_computation | async-start | bytes 16384 | tf_op jit(solution)/shard_map/all_to_all | solution.py:191
  48.4 24.9 %copy-start = (bf16[4,64,3072]{2,1,0:T(8,128)(2,1)}, bf16[4,64,3072]{2,1,0:T(8,128)(2,1)S(1)}, u32[]{:S(2)}) copy-start(bf16[4,64,3072]{2,1,0:T(8,128)(2,1)S(1)} %shard_map.57.refs_1_.refs_4_) | copy-start | bytes 4718596
  48.4 44.2 %collective-permute-start.8 = (bf16[4,64,3072]{2,1,0:T(8,128)(2,1)S(1)}, bf16[4,64,3072]{2,1,0:T(8,128)(2,1)}, u32[]{:S(2)}, u32[]{:S(2)}) collective-permute-start(bf16[4,64,3072]{2,1,0:T(8,128)(2,1)S(1)} %shard_map.57.refs_1_.refs_4_), channel_id=1, source_target_pairs={{0,2},{2,0},{1,3},{3,1},{4,6},{6,4},{5,7},{7,5},{8,10},{10,8},{9,1... | collective-permute-start | bytes 4718600 | tf_op jit(solution)/shard_map/ppermute | solution.py:193
  50.8 47.8 %copy-start.2 = (bf16[2,64,3072]{2,1,0:T(8,128)(2,1)}, bf16[2,64,3072]{2,1,0:T(8,128)(2,1)S(1)}, u32[]{:S(2)}) copy-start(bf16[2,64,3072]{2,1,0:T(8,128)(2,1)S(1)} %shard_map.58.refs_0_) | copy-start | bytes 2359300
  50.8 22.5 %collective-permute-start.5 = (bf16[2,64,3072]{2,1,0:T(8,128)(2,1)S(1)}, bf16[2,64,3072]{2,1,0:T(8,128)(2,1)S(1)}, u32[]{:S(2)}, u32[]{:S(2)}) collective-permute-start(bf16[2,64,3072]{2,1,0:T(8,128)(2,1)S(1)} %shard_map.58.refs_0_), channel_id=1, source_target_pairs={{0,4},{4,8},{8,12},{12,0},{1,5},{5,9},{9,13},{13,1},{2,6},{6,10},{... | collective-permute-start | bytes 2359304 | tf_op jit(solution)/shard_map/ppermute | solution.py:169
  53.3 49.9 %collective-permute-start.9 = (bf16[2,64,3072]{2,1,0:T(8,128)(2,1)S(1)}, bf16[2,64,3072]{2,1,0:T(8,128)(2,1)S(1)}, u32[]{:S(2)}, u32[]{:S(2)}) collective-permute-start(bf16[2,64,3072]{2,1,0:T(8,128)(2,1)S(1)} %shard_map.58.refs_0_), channel_id=1, source_target_pairs={{0,1},{1,0},{2,3},{3,2},{4,5},{5,4},{6,7},{7,6},{8,9},{9,8},{10,11... | collective-permute-start | bytes 2359304 | tf_op jit(solution)/shard_map/ppermute | solution.py:198
  56.0 45.2 %collective-permute-start.7 = (bf16[2,64,3072]{2,1,0:T(8,128)(2,1)S(1)}, bf16[2,64,3072]{2,1,0:T(8,128)(2,1)S(1)}, u32[]{:S(2)}, u32[]{:S(2)}) collective-permute-start(bf16[2,64,3072]{2,1,0:T(8,128)(2,1)S(1)} %shard_map.58.refs_0_), channel_id=1, source_target_pairs={{0,12},{4,0},{8,4},{12,8},{1,13},{5,1},{9,5},{13,9},{2,14},{6,2},{... | collective-permute-start | bytes 2359304 | tf_op jit(solution)/shard_map/ppermute | solution.py:169
  60.2 38.4 %collective-permute-start.6 = (bf16[2,64,3072]{2,1,0:T(8,128)(2,1)S(1)}, bf16[2,64,3072]{2,1,0:T(8,128)(2,1)}, u32[]{:S(2)}, u32[]{:S(2)}) collective-permute-start(bf16[2,64,3072]{2,1,0:T(8,128)(2,1)S(1)} %shard_map.58.refs_0_), channel_id=1, source_target_pairs={{0,8},{4,12},{8,0},{12,4},{1,9},{5,13},{9,1},{13,5},{2,10},{6,14},... | collective-permute-start | bytes 2359304 | tf_op jit(solution)/shard_map/ppermute | solution.py:169
  73.3 27.9 %copy-start.4 = (bf16[2,64,3072]{2,1,0:T(8,128)(2,1)}, bf16[2,64,3072]{2,1,0:T(8,128)(2,1)S(1)}, u32[]{:S(2)}) copy-start(bf16[2,64,3072]{2,1,0:T(8,128)(2,1)S(1)} %collective-permute-done.5.refs_1_) | copy-start | bytes 2359300
  73.3 34.7 %collective-permute-start.13 = (bf16[4,64,3072]{2,1,0:T(8,128)(2,1)S(1)}, bf16[4,64,3072]{2,1,0:T(8,128)(2,1)}, u32[]{:S(2)}, u32[]{:S(2)}) collective-permute-start(bf16[4,64,3072]{2,1,0:T(8,128)(2,1)S(1)} %shard_map.57.refs_1_.refs_4_), channel_id=1, source_target_pairs={{0,1},{1,0},{2,3},{3,2},{4,5},{5,4},{6,7},{7,6},{8,9},{9,8},{10,11... | collective-permute-start | bytes 4718600 | tf_op jit(solution)/shard_map/ppermute | solution.py:198
  92.6 16.0 %collective-permute-start.14 = (bf16[4,64,3072]{2,1,0:T(8,128)(2,1)}, bf16[4,64,3072]{2,1,0:T(8,128)(2,1)}, u32[]{:S(2)}, u32[]{:S(2)}) collective-permute-start(bf16[4,64,3072]{2,1,0:T(8,128)(2,1)} %collective-permute-done.8.refs_5_), channel_id=1, source_target_pairs={{0,1},{1,0},{2,3},{3,2},{4,5},{5,4},{6,7},{7,6},{8,9},{9,8},{10,11... | collective-permute-start | bytes 4718600 | tf_op jit(solution)/shard_map/ppermute | solution.py:198
  98.6 4.6 %copy-start.1 = (f32[2048,128]{1,0:T(8,128)}, f32[2048,128]{1,0:T(8,128)S(1)}, u32[]{:S(2)}) copy-start(f32[2048,128]{1,0:T(8,128)S(1)} %pad_maximum_fusion.1.refs_1_.refs_15_) | copy-start | bytes 3145732
  98.7 8.1 %copy-start.7 = (bf16[3,128]{1,0:T(4,128)(2,1)S(1)}, bf16[3,128]{1,0:T(4,128)(2,1)}, u32[]{:S(2)}) copy-start(bf16[3,128]{1,0:T(4,128)(2,1)} %param.8) | copy-start | bytes 2308
  98.7 9.4 %collective-permute-start.11 = (bf16[2,64,3072]{2,1,0:T(8,128)(2,1)}, bf16[2,64,3072]{2,1,0:T(8,128)(2,1)}, u32[]{:S(2)}, u32[]{:S(2)}) collective-permute-start(bf16[2,64,3072]{2,1,0:T(8,128)(2,1)} %shard_map.60.refs_2_), channel_id=1, source_target_pairs={{0,1},{1,0},{2,3},{3,2},{4,5},{5,4},{6,7},{7,6},{8,9},{9,8},{10,11... | collective-permute-start | bytes 2359304 | tf_op jit(solution)/shard_map/ppermute | solution.py:198
  101.2 6.8 %collective-permute-start.10 = (bf16[2,64,3072]{2,1,0:T(8,128)(2,1)S(1)}, bf16[2,64,3072]{2,1,0:T(8,128)(2,1)}, u32[]{:S(2)}, u32[]{:S(2)}) collective-permute-start(bf16[2,64,3072]{2,1,0:T(8,128)(2,1)S(1)} %collective-permute-done.5.refs_1_), channel_id=1, source_target_pairs={{0,1},{1,0},{2,3},{3,2},{4,5},{5,4},{6,7},{7,6},{8,9},{9,8},{10,11... | collective-permute-start | bytes 2359304 | tf_op jit(solution)/shard_map/ppermute | solution.py:198
  103.2 5.4 %copy-start.5 = (bf16[2,64,3072]{2,1,0:T(8,128)(2,1)}, bf16[2,64,3072]{2,1,0:T(8,128)(2,1)S(1)}, u32[]{:S(2)}) copy-start(bf16[2,64,3072]{2,1,0:T(8,128)(2,1)S(1)} %shard_map.61.refs_3_) | copy-start | bytes 2359300
  104.2 4.4 %collective-permute-start.12 = (bf16[2,64,3072]{2,1,0:T(8,128)(2,1)S(1)}, bf16[2,64,3072]{2,1,0:T(8,128)(2,1)}, u32[]{:S(2)}, u32[]{:S(2)}) collective-permute-start(bf16[2,64,3072]{2,1,0:T(8,128)(2,1)S(1)} %shard_map.61.refs_3_), channel_id=1, source_target_pairs={{0,1},{1,0},{2,3},{3,2},{4,5},{5,4},{6,7},{7,6},{8,9},{9,8},{10,11... | collective-permute-start | bytes 2359304 | tf_op jit(solution)/shard_map/ppermute | solution.py:198
  (3 other events, 3.0 us)
Sparse Core Ops, SparseCore 0:
  14.1 72.1 all-gather.1

commit v3 on v2

--- a/solution.py
+++ b/solution.py
@@ -189,17 +189,16 @@
     x_near = lax.ppermute(near, "x_hi", across)
     sent = jnp.broadcast_to(positions[None], (tensor, rows))
     places = lax.all_to_all(sent, ("y", "x_hi", "core"), 0, 0, tiled=True).reshape(-1)
-    far_own = gated(jnp.stack(along_y(far)), x_near, places)
+    far_own = gated(jnp.stack(along_y(far)), x_near)
     far_other = lax.ppermute(far_own, "x_hi", across)
-    near_all = along_y(gated(jnp.stack([near, x_near]), far_own))
-    turns = rotation(gated(places, near_all[1]))
-    near_all[2:] = [gated(piece, turns) for piece in near_all[2:]]
+    where = jnp.stack([lax.axis_index("x_hi"), lax.axis_index("core"), lax.axis_index("y")])
+    bias = key_bias.astype(jnp.float32).reshape(1, columns)
+    near_all = along_y(gated(jnp.stack([near, x_near]), far_own, where, bias))
+    turns = rotation(places)
     gathered = (*near_all, far_own, far_other)
     gathered += tuple(lax.ppermute(piece, "core", across) for piece in gathered)
-    where = jnp.stack([lax.axis_index("x_hi"), lax.axis_index("core"), lax.axis_index("y")])
 
     taps = jnp.transpose(conv_taps, (1, 0, 2)).reshape(conv_taps.shape[1], columns)
-    bias = key_bias.astype(jnp.float32).reshape(1, columns)
     keys = keys_of(where, gathered, weight, bias, taps, turns)
     return jnp.transpose(keys, (1, 0, 2))
 

time: 130 us -> 124 us (0.954)
  starting transfers between devices: 71.3 us -> 52.3 us
  waiting for transfers between devices: 18.7 us -> 34.2 us
  local copies, waits for them, and re-layouts: 4.15 us -> 2.27 us
    ppermute x1, waiting for transfers between devices: 0.01 us -> 20.8 us  [body(): far_other = lax.ppermute(far_own, 'x_hi', across)]
    ppermute x6, starting transfers between devices: 31 us -> 15.2 us  [body(): lax.ppermute(piece, 'core', across)]
    all_to_all x1, starting transfers between devices: 11.1 us -> 4.71 us  [body(): lax.all_to_all(sent, ('y', 'x_hi', 'core'), 0, 0, tiled=True).reshape(-1)]
    ppermute x1, starting transfers between devices: 2.27 us -> 6.92 us  [body(): far_other = lax.ppermute(far_own, 'x_hi', across)]
    all_to_all x1, waiting for transfers between devices: 5.02 us -> 0.39 us  [body(): lax.all_to_all(sent, ('y', 'x_hi', 'core'), 0, 0, tiled=True).reshape(-1)]
    unnamed x21 -> x19, local copies, waits for them, and re-layouts: 2.34 us -> 0.46 us
    ppermute x6, starting transfers between devices: 18.3 us -> 16.9 us  [step(): return lax.ppermute(value, 'y', [(i, (i + k) % Y) for i in range(Y)])]
  transfers between devices with their start and end apart: 17 -> 17, of which waited for: 4 -> 5; matrix products, arithmetic and copies ran while one was open for 6% -> 6% of each run, Pallas kernels for 0% -> 0%
where the time goes in v3:
time: 124 us; the launch traced here: 123 us
  starting transfers between devices  52.3 us (42%)
  waiting for transfers between devices  34.2 us (28%)
  between operations  13.8 us (11%)
  Pallas kernels  13.5 us (11%)
  other arithmetic  6.93 us (6%)
  local copies, waits for them, and re-layouts  2.27 us (2%)
    ppermute x1, waiting for transfers between devices, body(): far_other = lax.ppermute(far_own, 'x_hi', across)  20.8 us
    ppermute x6, starting transfers between devices, step(): return lax.ppermute(value, 'y', [(i, (i + k) % Y) for i in range(Y)])  16.9 us
    ppermute x6, starting transfers between devices, body(): lax.ppermute(piece, 'core', across)  15.2 us
    pallas_call x1, Pallas kernels, keys_of(): pl.pallas_call(keys_kernel, in_specs=[pl.BlockSpec(memory_space=pltpu.SME...  13.5 us
    ppermute x6, waiting for transfers between devices, step(): return lax.ppermute(value, 'y', [(i, (i + k) % Y) for i in range(Y)])  11.1 us
    ppermute x1, starting transfers between devices, body(): far_other = lax.ppermute(far_own, 'x_hi', across)  6.92 us
    all_to_all x1, starting transfers between devices, body(): lax.all_to_all(sent, ('y', 'x_hi', 'core'), 0, 0, tiled=True).reshape(-1)  4.71 us
    ppermute x1, starting transfers between devices, body(): x_near = lax.ppermute(near, 'x_hi', across)  4.65 us
  transfers between devices with their start and end apart: 17, of which 5 were waited for; matrix products, arithmetic and copies ran while one was open for 6% of the time, Pallas kernels for 0%

profile of v3, /device:TPU:1, one launch (start us, length us, event | category | flops | bytes accessed | tf_op | source)
XLA Modules:
  0.0 123.0 jit_solution(6675576479703423065)
XLA Ops:
  6.5 3.9 %collective-permute-start = (bf16[3,96,128]{2,1,0:T(8,128)(2,1)}, bf16[3,96,128]{2,1,0:T(8,128)(2,1)S(1)}, u32[]{:S(2)}, u32[]{:S(2)}) collective-permute-start(bf16[3,96,128]{2,1,0:T(8,128)(2,1)} %bitcast.36), channel_id=1, source_target_pairs={{0,16},{16,0},{1,17},{17,1},{2,18},{18,2},{3,19},{19,3},{4,20},{20... | collective-permute-start | bytes 221192 | tf_op jit(solution)/shard_map/ppermute | solution.py:180
  10.5 1.9 %collective-permute-done = bf16[3,96,128]{2,1,0:T(8,128)(2,1)S(1)} collective-permute-done((bf16[3,96,128]{2,1,0:T(8,128)(2,1)}, bf16[3,96,128]{2,1,0:T(8,128)(2,1)S(1)}, u32[]{:S(2)}, u32[]{:S(2)}) %collective-permute-start) | collective-permute-done | bytes 73760 | tf_op jit(solution)/shard_map/ppermute | solution.py:180
  12.4 0.9 broadcast_select_fusion.1
  14.0 1.2 fusion
  15.3 4.9 %collective-permute-start.4 = (bf16[64,3072]{1,0:T(8,128)(2,1)S(1)}, bf16[64,3072]{1,0:T(8,128)(2,1)S(1)}, u32[]{:S(2)}, u32[]{:S(2)}) collective-permute-start(bf16[64,3072]{1,0:T(8,128)(2,1)S(1)} %shard_map.56), channel_id=1, source_target_pairs={{0,12},{4,0},{8,4},{12,8},{1,13},{5,1},{9,5},{13,9},{2,14},{6,2},{... | collective-permute-start | bytes 1179656 | tf_op jit(solution)/shard_map/ppermute | solution.py:169
  20.1 2.3 %collective-permute-start.3 = (bf16[64,3072]{1,0:T(8,128)(2,1)S(1)}, bf16[64,3072]{1,0:T(8,128)(2,1)S(1)}, u32[]{:S(2)}, u32[]{:S(2)}) collective-permute-start(bf16[64,3072]{1,0:T(8,128)(2,1)S(1)} %shard_map.56), channel_id=1, source_target_pairs={{0,8},{4,12},{8,0},{12,4},{1,9},{5,13},{9,1},{13,5},{2,10},{6,14},... | collective-permute-start | bytes 1179656 | tf_op jit(solution)/shard_map/ppermute | solution.py:169
  22.4 2.6 %collective-permute-start.2 = (bf16[64,3072]{1,0:T(8,128)(2,1)S(1)}, bf16[64,3072]{1,0:T(8,128)(2,1)S(1)}, u32[]{:S(2)}, u32[]{:S(2)}) collective-permute-start(bf16[64,3072]{1,0:T(8,128)(2,1)S(1)} %shard_map.56), channel_id=1, source_target_pairs={{0,4},{4,8},{8,12},{12,0},{1,5},{5,9},{9,13},{13,1},{2,6},{6,10},{... | collective-permute-start | bytes 1179656 | tf_op jit(solution)/shard_map/ppermute | solution.py:169
  25.0 4.7 %collective-permute-start.1 = (bf16[64,3072]{1,0:T(8,128)(2,1)S(1)}, bf16[64,3072]{1,0:T(8,128)(2,1)S(1)}, u32[]{:S(2)}, u32[]{:S(2)}) collective-permute-start(bf16[64,3072]{1,0:T(8,128)(2,1)S(1)} %shard_map.55), channel_id=1, source_target_pairs={{0,2},{2,0},{1,3},{3,1},{4,6},{6,4},{5,7},{7,5},{8,10},{10,8},{9,1... | collective-permute-start | bytes 1179656 | tf_op jit(solution)/shard_map/ppermute | solution.py:189
  30.4 10.3 %collective-permute-done.2 = bf16[64,3072]{1,0:T(8,128)(2,1)S(1)} collective-permute-done((bf16[64,3072]{1,0:T(8,128)(2,1)S(1)}, bf16[64,3072]{1,0:T(8,128)(2,1)S(1)}, u32[]{:S(2)}, u32[]{:S(2)}) %collective-permute-start.2) | collective-permute-done | bytes 393248 | tf_op jit(solution)/shard_map/ppermute | solution.py:169
  41.0 6.9 %collective-permute-start.8 = (bf16[4,64,3072]{2,1,0:T(8,128)(2,1)S(1)}, bf16[4,64,3072]{2,1,0:T(8,128)(2,1)}, u32[]{:S(2)}, u32[]{:S(2)}) collective-permute-start(bf16[4,64,3072]{2,1,0:T(8,128)(2,1)S(1)} %shard_map.57.refs_1_.refs_4_), channel_id=1, source_target_pairs={{0,2},{2,0},{1,3},{3,1},{4,6},{6,4},{5,7},{7,5},{8,10},{10,8},{9,1... | collective-permute-start | bytes 4718600 | tf_op jit(solution)/shard_map/ppermute | solution.py:193
  48.6 2.7 %collective-permute-start.9 = (bf16[2,64,3072]{2,1,0:T(8,128)(2,1)S(1)}, bf16[2,64,3072]{2,1,0:T(8,128)(2,1)S(1)}, u32[]{:S(2)}, u32[]{:S(2)}) collective-permute-start(bf16[2,64,3072]{2,1,0:T(8,128)(2,1)S(1)} %shard_map.58.refs_0_), channel_id=1, source_target_pairs={{0,1},{1,0},{2,3},{3,2},{4,5},{5,4},{6,7},{7,6},{8,9},{9,8},{10,11... | collective-permute-start | bytes 2359304 | tf_op jit(solution)/shard_map/ppermute | solution.py:199
  51.2 2.2 %collective-permute-start.7 = (bf16[2,64,3072]{2,1,0:T(8,128)(2,1)S(1)}, bf16[2,64,3072]{2,1,0:T(8,128)(2,1)S(1)}, u32[]{:S(2)}, u32[]{:S(2)}) collective-permute-start(bf16[2,64,3072]{2,1,0:T(8,128)(2,1)S(1)} %shard_map.58.refs_0_), channel_id=1, source_target_pairs={{0,12},{4,0},{8,4},{12,8},{1,13},{5,1},{9,5},{13,9},{2,14},{6,2},{... | collective-permute-start | bytes 2359304 | tf_op jit(solution)/shard_map/ppermute | solution.py:169
  53.5 2.3 %collective-permute-start.6 = (bf16[2,64,3072]{2,1,0:T(8,128)(2,1)S(1)}, bf16[2,64,3072]{2,1,0:T(8,128)(2,1)}, u32[]{:S(2)}, u32[]{:S(2)}) collective-permute-start(bf16[2,64,3072]{2,1,0:T(8,128)(2,1)S(1)} %shard_map.58.refs_0_), channel_id=1, source_target_pairs={{0,8},{4,12},{8,0},{12,4},{1,9},{5,13},{9,1},{13,5},{2,10},{6,14},... | collective-permute-start | bytes 2359304 | tf_op jit(solution)/shard_map/ppermute | solution.py:169
  55.8 2.7 %collective-permute-start.5 = (bf16[2,64,3072]{2,1,0:T(8,128)(2,1)S(1)}, bf16[2,64,3072]{2,1,0:T(8,128)(2,1)}, u32[]{:S(2)}, u32[]{:S(2)}) collective-permute-start(bf16[2,64,3072]{2,1,0:T(8,128)(2,1)S(1)} %shard_map.58.refs_0_), channel_id=1, source_target_pairs={{0,4},{4,8},{8,12},{12,0},{1,5},{5,9},{9,13},{13,1},{2,6},{6,10},{... | collective-permute-start | bytes 2359304 | tf_op jit(solution)/shard_map/ppermute | solution.py:169
  58.5 2.5 %collective-permute-start.13 = (bf16[4,64,3072]{2,1,0:T(8,128)(2,1)S(1)}, bf16[4,64,3072]{2,1,0:T(8,128)(2,1)}, u32[]{:S(2)}, u32[]{:S(2)}) collective-permute-start(bf16[4,64,3072]{2,1,0:T(8,128)(2,1)S(1)} %shard_map.57.refs_1_.refs_4_), channel_id=1, source_target_pairs={{0,1},{1,0},{2,3},{3,2},{4,5},{5,4},{6,7},{7,6},{8,9},{9,8},{10,11... | collective-permute-start | bytes 4718600 | tf_op jit(solution)/shard_map/ppermute | solution.py:199
  61.0 20.8 %collective-permute-done.8.refs_5_ = bf16[4,64,3072]{2,1,0:T(8,128)(2,1)} collective-permute-done((bf16[4,64,3072]{2,1,0:T(8,128)(2,1)S(1)}, bf16[4,64,3072]{2,1,0:T(8,128)(2,1)}, u32[]{:S(2)}, u32[]{:S(2)}) %collective-permute-start.8) | collective-permute-done | bytes 1572896 | tf_op jit(solution)/shard_map/ppermute | solution.py:193
  81.8 3.5 %collective-permute-start.14 = (bf16[4,64,3072]{2,1,0:T(8,128)(2,1)}, bf16[4,64,3072]{2,1,0:T(8,128)(2,1)}, u32[]{:S(2)}, u32[]{:S(2)}) collective-permute-start(bf16[4,64,3072]{2,1,0:T(8,128)(2,1)} %collective-permute-done.8.refs_5_), channel_id=1, source_target_pairs={{0,1},{1,0},{2,3},{3,2},{4,5},{5,4},{6,7},{7,6},{8,9},{9,8},{10,11... | collective-permute-start | bytes 4718600 | tf_op jit(solution)/shard_map/ppermute | solution.py:199
  85.9 4.7 %all-to-all-start = ((s32[16,1,128]{2,1,0:T(1,128)}), s32[16,1,128]{2,1,0:T(1,128)S(1)}, u32[]{:S(2)}, u32[]{:S(2)}) async-start(s32[16,1,128]{2,1,0:T(1,128)} %broadcast_in_dim.2), calls=%async_computation | async-start | bytes 16384 | tf_op jit(solution)/shard_map/all_to_all | solution.py:191
  90.6 2.0 %collective-permute-start.12 = (bf16[2,64,3072]{2,1,0:T(8,128)(2,1)S(1)}, bf16[2,64,3072]{2,1,0:T(8,128)(2,1)}, u32[]{:S(2)}, u32[]{:S(2)}) collective-permute-start(bf16[2,64,3072]{2,1,0:T(8,128)(2,1)S(1)} %collective-permute-done.7.refs_3_), channel_id=1, source_target_pairs={{0,1},{1,0},{2,3},{3,2},{4,5},{5,4},{6,7},{7,6},{8,9},{9,8},{10,11... | collective-permute-start | bytes 2359304 | tf_op jit(solution)/shard_map/ppermute | solution.py:199
  92.6 2.3 %collective-permute-start.11 = (bf16[2,64,3072]{2,1,0:T(8,128)(2,1)}, bf16[2,64,3072]{2,1,0:T(8,128)(2,1)}, u32[]{:S(2)}, u32[]{:S(2)}) collective-permute-start(bf16[2,64,3072]{2,1,0:T(8,128)(2,1)} %collective-permute-done.6.refs_2_), channel_id=1, source_target_pairs={{0,1},{1,0},{2,3},{3,2},{4,5},{5,4},{6,7},{7,6},{8,9},{9,8},{10,11... | collective-permute-start | bytes 2359304 | tf_op jit(solution)/shard_map/ppermute | solution.py:199
  95.0 2.2 %collective-permute-start.10 = (bf16[2,64,3072]{2,1,0:T(8,128)(2,1)}, bf16[2,64,3072]{2,1,0:T(8,128)(2,1)}, u32[]{:S(2)}, u32[]{:S(2)}) collective-permute-start(bf16[2,64,3072]{2,1,0:T(8,128)(2,1)} %collective-permute-done.5.refs_1_), channel_id=1, source_target_pairs={{0,1},{1,0},{2,3},{3,2},{4,5},{5,4},{6,7},{7,6},{8,9},{9,8},{10,11... | collective-permute-start | bytes 2359304 | tf_op jit(solution)/shard_map/ppermute | solution.py:199
  97.6 3.7 %multiply_cosine_fusion = (f32[2048,64]{1,0:T(8,128)S(1)}, f32[2048,64]{1,0:T(8,128)S(1)}) fusion(f32[64]{0:T(128)S(1)} %multiply_power_fusion, f32[2048]{0:T(1024)S(1)} %bitcast.37), kind=kLoop, calls=%fused_computation.2 | loop fusion | flops 131072 | bytes 1057024 | tf_op jit(solution)/shard_map/cos | solution.py:133
  101.3 1.3 %pad_maximum_fusion.1.refs_15_ = f32[2048,128]{1,0:T(8,128)} fusion(f32[2048,64]{1,0:T(8,128)S(1)} %get-tuple-element.10, f32[2048,64]{1,0:T(8,128)S(1)} %get-tuple-element.9), kind=kLoop, calls=%fused_computation.3 | loop fusion | flops 262144 | bytes 2097152 | tf_op jit(solution)/shard_map/concatenate | solution.py:133
  102.6 13.5 %shard_map.59 = bf16[3,2048,128]{2,1,0:T(8,128)(2,1)} custom-call(s32[3]{0:T(128)} %copy-done.4, bf16[2,64,3072]{2,1,0:T(8,128)(2,1)} %copy-done.1, bf16[2,64,3072]{2,1,0:T(8,128)(2,1)} %collective-permute-done.5.refs_1_, bf16[2,64,3072]{2,1,0:T(8,128)(2,1)} %collective-permute-done.6.refs_2_, bf16[2,64,3072]{2,1,0:T(8,128)(2,1)} %copy-done.8, ...), custom_call_target="tpu_custom_call" | custom-call | flops 4831838208 | bytes 16515072 | tf_op jit(solution)/shard_map/pallas_call | solution.py:143
  (47 shorter events, 3.3 us)
Async XLA Ops:
  6.5 96.1 %all-gather.2.cloned.1.call-start = ((), (), s32[]{:S(2)}) async-start(), calls=%async_computation.1 | async-start | bytes 2506752 | tf_op jit(solution)/shard_map/all_gather | solution.py:185
  6.5 5.9 %collective-permute-start = (bf16[3,96,128]{2,1,0:T(8,128)(2,1)}, bf16[3,96,128]{2,1,0:T(8,128)(2,1)S(1)}, u32[]{:S(2)}, u32[]{:S(2)}) collective-permute-start(bf16[3,96,128]{2,1,0:T(8,128)(2,1)} %bitcast.36), channel_id=1, source_target_pairs={{0,16},{16,0},{1,17},{17,1},{2,18},{18,2},{3,19},{19,3},{4,20},{20... | collective-permute-start | bytes 221192 | tf_op jit(solution)/shard_map/ppermute | solution.py:180
  14.0 1.2 %copy-start.2 = (bf16[3,192,128]{2,1,0:T(8,128)(2,1)S(1)}, bf16[3,192,128]{2,1,0:T(8,128)(2,1)}, u32[]{:S(2)}) copy-start(bf16[3,192,128]{2,1,0:T(8,128)(2,1)} %pad_maximum_fusion.3) | copy-start | bytes 442372
  15.3 15.2 %collective-permute-start.4 = (bf16[64,3072]{1,0:T(8,128)(2,1)S(1)}, bf16[64,3072]{1,0:T(8,128)(2,1)S(1)}, u32[]{:S(2)}, u32[]{:S(2)}) collective-permute-start(bf16[64,3072]{1,0:T(8,128)(2,1)S(1)} %shard_map.56), channel_id=1, source_target_pairs={{0,12},{4,0},{8,4},{12,8},{1,13},{5,1},{9,5},{13,9},{2,14},{6,2},{... | collective-permute-start | bytes 1179656 | tf_op jit(solution)/shard_map/ppermute | solution.py:169
  20.1 10.3 %collective-permute-start.3 = (bf16[64,3072]{1,0:T(8,128)(2,1)S(1)}, bf16[64,3072]{1,0:T(8,128)(2,1)S(1)}, u32[]{:S(2)}, u32[]{:S(2)}) collective-permute-start(bf16[64,3072]{1,0:T(8,128)(2,1)S(1)} %shard_map.56), channel_id=1, source_target_pairs={{0,8},{4,12},{8,0},{12,4},{1,9},{5,13},{9,1},{13,5},{2,10},{6,14},... | collective-permute-start | bytes 1179656 | tf_op jit(solution)/shard_map/ppermute | solution.py:169
  22.4 18.3 %collective-permute-start.2 = (bf16[64,3072]{1,0:T(8,128)(2,1)S(1)}, bf16[64,3072]{1,0:T(8,128)(2,1)S(1)}, u32[]{:S(2)}, u32[]{:S(2)}) collective-permute-start(bf16[64,3072]{1,0:T(8,128)(2,1)S(1)} %shard_map.56), channel_id=1, source_target_pairs={{0,4},{4,8},{8,12},{12,0},{1,5},{5,9},{9,13},{13,1},{2,6},{6,10},{... | collective-permute-start | bytes 1179656 | tf_op jit(solution)/shard_map/ppermute | solution.py:169
  25.0 15.9 %collective-permute-start.1 = (bf16[64,3072]{1,0:T(8,128)(2,1)S(1)}, bf16[64,3072]{1,0:T(8,128)(2,1)S(1)}, u32[]{:S(2)}, u32[]{:S(2)}) collective-permute-start(bf16[64,3072]{1,0:T(8,128)(2,1)S(1)} %shard_map.55), channel_id=1, source_target_pairs={{0,2},{2,0},{1,3},{3,1},{4,6},{6,4},{5,7},{7,5},{8,10},{10,8},{9,1... | collective-permute-start | bytes 1179656 | tf_op jit(solution)/shard_map/ppermute | solution.py:189
  40.9 7.0 %copy-start.5 = (bf16[3,128]{1,0:T(4,128)(2,1)S(1)}, bf16[3,128]{1,0:T(4,128)(2,1)}, u32[]{:S(2)}) copy-start(bf16[3,128]{1,0:T(4,128)(2,1)} %param.8) | copy-start | bytes 2308
  41.0 17.5 %copy-start = (bf16[4,64,3072]{2,1,0:T(8,128)(2,1)}, bf16[4,64,3072]{2,1,0:T(8,128)(2,1)S(1)}, u32[]{:S(2)}) copy-start(bf16[4,64,3072]{2,1,0:T(8,128)(2,1)S(1)} %shard_map.57.refs_1_.refs_4_) | copy-start | bytes 4718596
  41.0 40.8 %collective-permute-start.8 = (bf16[4,64,3072]{2,1,0:T(8,128)(2,1)S(1)}, bf16[4,64,3072]{2,1,0:T(8,128)(2,1)}, u32[]{:S(2)}, u32[]{:S(2)}) collective-permute-start(bf16[4,64,3072]{2,1,0:T(8,128)(2,1)S(1)} %shard_map.57.refs_1_.refs_4_), channel_id=1, source_target_pairs={{0,2},{2,0},{1,3},{3,1},{4,6},{6,4},{5,7},{7,5},{8,10},{10,8},{9,1... | collective-permute-start | bytes 4718600 | tf_op jit(solution)/shard_map/ppermute | solution.py:193
  48.1 37.1 %copy-start.6 = (s32[128]{0:T(128)S(1)}, s32[128]{0:T(128)}, u32[]{:S(2)}) copy-start(s32[128]{0:T(128)} %param.6) | copy-start | bytes 1540
  48.6 54.0 %copy-start.1 = (bf16[2,64,3072]{2,1,0:T(8,128)(2,1)}, bf16[2,64,3072]{2,1,0:T(8,128)(2,1)S(1)}, u32[]{:S(2)}) copy-start(bf16[2,64,3072]{2,1,0:T(8,128)(2,1)S(1)} %shard_map.58.refs_0_) | copy-start | bytes 2359300
  48.6 9.9 %collective-permute-start.9 = (bf16[2,64,3072]{2,1,0:T(8,128)(2,1)S(1)}, bf16[2,64,3072]{2,1,0:T(8,128)(2,1)S(1)}, u32[]{:S(2)}, u32[]{:S(2)}) collective-permute-start(bf16[2,64,3072]{2,1,0:T(8,128)(2,1)S(1)} %shard_map.58.refs_0_), channel_id=1, source_target_pairs={{0,1},{1,0},{2,3},{3,2},{4,5},{5,4},{6,7},{7,6},{8,9},{9,8},{10,11... | collective-permute-start | bytes 2359304 | tf_op jit(solution)/shard_map/ppermute | solution.py:199
  51.2 39.3 %collective-permute-start.7 = (bf16[2,64,3072]{2,1,0:T(8,128)(2,1)S(1)}, bf16[2,64,3072]{2,1,0:T(8,128)(2,1)S(1)}, u32[]{:S(2)}, u32[]{:S(2)}) collective-permute-start(bf16[2,64,3072]{2,1,0:T(8,128)(2,1)S(1)} %shard_map.58.refs_0_), channel_id=1, source_target_pairs={{0,12},{4,0},{8,4},{12,8},{1,13},{5,1},{9,5},{13,9},{2,14},{6,2},{... | collective-permute-start | bytes 2359304 | tf_op jit(solution)/shard_map/ppermute | solution.py:169
  53.5 39.1 %collective-permute-start.6 = (bf16[2,64,3072]{2,1,0:T(8,128)(2,1)S(1)}, bf16[2,64,3072]{2,1,0:T(8,128)(2,1)}, u32[]{:S(2)}, u32[]{:S(2)}) collective-permute-start(bf16[2,64,3072]{2,1,0:T(8,128)(2,1)S(1)} %shard_map.58.refs_0_), channel_id=1, source_target_pairs={{0,8},{4,12},{8,0},{12,4},{1,9},{5,13},{9,1},{13,5},{2,10},{6,14},... | collective-permute-start | bytes 2359304 | tf_op jit(solution)/shard_map/ppermute | solution.py:169
  55.8 39.2 %collective-permute-start.5 = (bf16[2,64,3072]{2,1,0:T(8,128)(2,1)S(1)}, bf16[2,64,3072]{2,1,0:T(8,128)(2,1)}, u32[]{:S(2)}, u32[]{:S(2)}) collective-permute-start(bf16[2,64,3072]{2,1,0:T(8,128)(2,1)S(1)} %shard_map.58.refs_0_), channel_id=1, source_target_pairs={{0,4},{4,8},{8,12},{12,0},{1,5},{5,9},{9,13},{13,1},{2,6},{6,10},{... | collective-permute-start | bytes 2359304 | tf_op jit(solution)/shard_map/ppermute | solution.py:169
  58.5 23.3 %copy-start.7 = (bf16[2,64,3072]{2,1,0:T(8,128)(2,1)}, bf16[2,64,3072]{2,1,0:T(8,128)(2,1)S(1)}, u32[]{:S(2)}) copy-start(bf16[2,64,3072]{2,1,0:T(8,128)(2,1)S(1)} %collective-permute-done.9.refs_6_) | copy-start | bytes 2359300
  58.5 44.1 %collective-permute-start.13 = (bf16[4,64,3072]{2,1,0:T(8,128)(2,1)S(1)}, bf16[4,64,3072]{2,1,0:T(8,128)(2,1)}, u32[]{:S(2)}, u32[]{:S(2)}) collective-permute-start(bf16[4,64,3072]{2,1,0:T(8,128)(2,1)S(1)} %shard_map.57.refs_1_.refs_4_), channel_id=1, source_target_pairs={{0,1},{1,0},{2,3},{3,2},{4,5},{5,4},{6,7},{7,6},{8,9},{9,8},{10,11... | collective-permute-start | bytes 4718600 | tf_op jit(solution)/shard_map/ppermute | solution.py:199
  81.8 20.8 %collective-permute-start.14 = (bf16[4,64,3072]{2,1,0:T(8,128)(2,1)}, bf16[4,64,3072]{2,1,0:T(8,128)(2,1)}, u32[]{:S(2)}, u32[]{:S(2)}) collective-permute-start(bf16[4,64,3072]{2,1,0:T(8,128)(2,1)} %collective-permute-done.8.refs_5_), channel_id=1, source_target_pairs={{0,1},{1,0},{2,3},{3,2},{4,5},{5,4},{6,7},{7,6},{8,9},{9,8},{10,11... | collective-permute-start | bytes 4718600 | tf_op jit(solution)/shard_map/ppermute | solution.py:199
  85.9 11.7 %all-to-all-start = ((s32[16,1,128]{2,1,0:T(1,128)}), s32[16,1,128]{2,1,0:T(1,128)S(1)}, u32[]{:S(2)}, u32[]{:S(2)}) async-start(s32[16,1,128]{2,1,0:T(1,128)} %broadcast_in_dim.2), calls=%async_computation | async-start | bytes 16384 | tf_op jit(solution)/shard_map/all_to_all | solution.py:191
  90.6 12.0 %copy-start.8 = (bf16[2,64,3072]{2,1,0:T(8,128)(2,1)}, bf16[2,64,3072]{2,1,0:T(8,128)(2,1)S(1)}, u32[]{:S(2)}) copy-start(bf16[2,64,3072]{2,1,0:T(8,128)(2,1)S(1)} %collective-permute-done.7.refs_3_) | copy-start | bytes 2359300
  90.6 12.0 %collective-permute-start.12 = (bf16[2,64,3072]{2,1,0:T(8,128)(2,1)S(1)}, bf16[2,64,3072]{2,1,0:T(8,128)(2,1)}, u32[]{:S(2)}, u32[]{:S(2)}) collective-permute-start(bf16[2,64,3072]{2,1,0:T(8,128)(2,1)S(1)} %collective-permute-done.7.refs_3_), channel_id=1, source_target_pairs={{0,1},{1,0},{2,3},{3,2},{4,5},{5,4},{6,7},{7,6},{8,9},{9,8},{10,11... | collective-permute-start | bytes 2359304 | tf_op jit(solution)/shard_map/ppermute | solution.py:199
  92.6 10.0 %collective-permute-start.11 = (bf16[2,64,3072]{2,1,0:T(8,128)(2,1)}, bf16[2,64,3072]{2,1,0:T(8,128)(2,1)}, u32[]{:S(2)}, u32[]{:S(2)}) collective-permute-start(bf16[2,64,3072]{2,1,0:T(8,128)(2,1)} %collective-permute-done.6.refs_2_), channel_id=1, source_target_pairs={{0,1},{1,0},{2,3},{3,2},{4,5},{5,4},{6,7},{7,6},{8,9},{9,8},{10,11... | collective-permute-start | bytes 2359304 | tf_op jit(solution)/shard_map/ppermute | solution.py:199
  95.0 7.6 %collective-permute-start.10 = (bf16[2,64,3072]{2,1,0:T(8,128)(2,1)}, bf16[2,64,3072]{2,1,0:T(8,128)(2,1)}, u32[]{:S(2)}, u32[]{:S(2)}) collective-permute-start(bf16[2,64,3072]{2,1,0:T(8,128)(2,1)} %collective-permute-done.5.refs_1_), channel_id=1, source_target_pairs={{0,1},{1,0},{2,3},{3,2},{4,5},{5,4},{6,7},{7,6},{8,9},{9,8},{10,11... | collective-permute-start | bytes 2359304 | tf_op jit(solution)/shard_map/ppermute | solution.py:199
  (2 other events, 1.1 us)
Sparse Core Ops, SparseCore 0:
  14.1 72.0 all-gather.1

commit v4 on v3

--- a/solution.py
+++ b/solution.py
@@ -187,16 +187,18 @@
     across = [(0, 1), (1, 0)]
     near, far = gated(tokens[:NEAR], pair), gated(tokens[NEAR:], pair)
     x_near = lax.ppermute(near, "x_hi", across)
-    sent = jnp.broadcast_to(positions[None], (tensor, rows))
-    places = lax.all_to_all(sent, ("y", "x_hi", "core"), 0, 0, tiled=True).reshape(-1)
     far_own = gated(jnp.stack(along_y(far)), x_near)
     far_other = lax.ppermute(far_own, "x_hi", across)
     where = jnp.stack([lax.axis_index("x_hi"), lax.axis_index("core"), lax.axis_index("y")])
     bias = key_bias.astype(jnp.float32).reshape(1, columns)
     near_all = along_y(gated(jnp.stack([near, x_near]), far_own, where, bias))
+    x_first = lax.ppermute(near_all[0], "core", across)
+    sent = gated(jnp.broadcast_to(positions[None], (tensor, rows)), x_first)
+    places = lax.all_to_all(sent, ("y", "x_hi", "core"), 0, 0, tiled=True).reshape(-1)
     turns = rotation(places)
+    far_other = gated(far_other, places)
     gathered = (*near_all, far_own, far_other)
-    gathered += tuple(lax.ppermute(piece, "core", across) for piece in gathered)
+    gathered += (x_first, *(lax.ppermute(piece, "core", across) for piece in gathered[1:]))
 
     taps = jnp.transpose(conv_taps, (1, 0, 2)).reshape(conv_taps.shape[1], columns)
     keys = keys_of(where, gathered, weight, bias, taps, turns)

time: 124 us -> 130 us (1.048)
  waiting for transfers between devices: 34.2 us -> 36.6 us
  starting transfers between devices: 52.3 us -> 54.4 us
  local copies, waits for them, and re-layouts: 2.27 us -> 3.73 us
    all_to_all x1, waiting for transfers between devices: 0.39 us -> 25.7 us  [body(): lax.all_to_all(sent, ('y', 'x_hi', 'core'), 0, 0, tiled=True).reshape(-1)]
    ppermute x1, waiting for transfers between devices: 20.8 us -> 0.01 us  [body(): far_other = lax.ppermute(far_own, 'x_hi', across)]
    ppermute x0 -> x1, starting transfers between devices: none -> 6.19 us  [body(): x_first = lax.ppermute(near_all[0], 'core', across)]
    ppermute x6 -> x5, starting transfers between devices: 15.2 us -> 10.8 us  [body(): lax.ppermute(piece, 'core', across)]
    ppermute x1, starting transfers between devices: 6.92 us -> 4.66 us  [body(): far_other = lax.ppermute(far_own, 'x_hi', across)]
    ppermute x6, waiting for transfers between devices: 11.1 us -> 8.89 us  [step(): return lax.ppermute(value, 'y', [(i, (i + k) % Y) for i in range(Y)])]
    ppermute x6, starting transfers between devices: 16.9 us -> 18.8 us  [step(): return lax.ppermute(value, 'y', [(i, (i + k) % Y) for i in range(Y)])]
    unnamed x19 -> x23, local copies, waits for them, and re-layouts: 0.46 us -> 1.86 us
  transfers between devices with their start and end apart: 17 -> 17, of which waited for: 5 -> 3; matrix products, arithmetic and copies ran while one was open for 6% -> 6% of each run, Pallas kernels for 0% -> 0%
where the time goes in v4:
time: 130 us; the launch traced here: 129 us
  starting transfers between devices  54.4 us (42%)
  waiting for transfers between devices  36.6 us (28%)
  between operations  13.8 us (11%)
  Pallas kernels  13.5 us (10%)
  other arithmetic  6.94 us (5%)
  local copies, waits for them, and re-layouts  3.73 us (3%)
    all_to_all x1, waiting for transfers between devices, body(): lax.all_to_all(sent, ('y', 'x_hi', 'core'), 0, 0, tiled=True).reshape(-1)  25.7 us
    ppermute x6, starting transfers between devices, step(): return lax.ppermute(value, 'y', [(i, (i + k) % Y) for i in range(Y)])  18.8 us
    pallas_call x1, Pallas kernels, keys_of(): pl.pallas_call(keys_kernel, in_specs=[pl.BlockSpec(memory_space=pltpu.SME...  13.5 us
    ppermute x5, starting transfers between devices, body(): lax.ppermute(piece, 'core', across)  10.8 us
    ppermute x6, waiting for transfers between devices, step(): return lax.ppermute(value, 'y', [(i, (i + k) % Y) for i in range(Y)])  8.89 us
    ppermute x1, starting transfers between devices, body(): x_first = lax.ppermute(near_all[0], 'core', across)  6.19 us
    all_to_all x1, starting transfers between devices, body(): lax.all_to_all(sent, ('y', 'x_hi', 'core'), 0, 0, tiled=True).reshape(-1)  5.35 us
    ppermute x1, starting transfers between devices, body(): far_other = lax.ppermute(far_own, 'x_hi', across)  4.66 us
  transfers between devices with their start and end apart: 17, of which 3 were waited for; matrix products, arithmetic and copies ran while one was open for 6% of the time, Pallas kernels for 0%

profile of v4, /device:TPU:1, one launch (start us, length us, event | category | flops | bytes accessed | tf_op | source)
XLA Modules:
  0.0 128.9 jit_solution(1744051394999540173)
XLA Ops:
  6.5 3.9 %collective-permute-start = (bf16[3,96,128]{2,1,0:T(8,128)(2,1)}, bf16[3,96,128]{2,1,0:T(8,128)(2,1)S(1)}, u32[]{:S(2)}, u32[]{:S(2)}) collective-permute-start(bf16[3,96,128]{2,1,0:T(8,128)(2,1)} %bitcast.41), channel_id=1, source_target_pairs={{0,16},{16,0},{1,17},{17,1},{2,18},{18,2},{3,19},{19,3},{4,20},{20... | collective-permute-start | bytes 221192 | tf_op jit(solution)/shard_map/ppermute | solution.py:180
  10.5 1.9 %collective-permute-done = bf16[3,96,128]{2,1,0:T(8,128)(2,1)S(1)} collective-permute-done((bf16[3,96,128]{2,1,0:T(8,128)(2,1)}, bf16[3,96,128]{2,1,0:T(8,128)(2,1)S(1)}, u32[]{:S(2)}, u32[]{:S(2)}) %collective-permute-start) | collective-permute-done | bytes 73760 | tf_op jit(solution)/shard_map/ppermute | solution.py:180
  12.4 0.9 broadcast_select_fusion.1
  14.0 1.2 fusion
  15.3 4.9 %collective-permute-start.4 = (bf16[64,3072]{1,0:T(8,128)(2,1)S(1)}, bf16[64,3072]{1,0:T(8,128)(2,1)S(1)}, u32[]{:S(2)}, u32[]{:S(2)}) collective-permute-start(bf16[64,3072]{1,0:T(8,128)(2,1)S(1)} %shard_map.56), channel_id=1, source_target_pairs={{0,12},{4,0},{8,4},{12,8},{1,13},{5,1},{9,5},{13,9},{2,14},{6,2},{... | collective-permute-start | bytes 1179656 | tf_op jit(solution)/shard_map/ppermute | solution.py:169
  20.1 1.9 %collective-permute-start.2 = (bf16[64,3072]{1,0:T(8,128)(2,1)S(1)}, bf16[64,3072]{1,0:T(8,128)(2,1)S(1)}, u32[]{:S(2)}, u32[]{:S(2)}) collective-permute-start(bf16[64,3072]{1,0:T(8,128)(2,1)S(1)} %shard_map.56), channel_id=1, source_target_pairs={{0,4},{4,8},{8,12},{12,0},{1,5},{5,9},{9,13},{13,1},{2,6},{6,10},{... | collective-permute-start | bytes 1179656 | tf_op jit(solution)/shard_map/ppermute | solution.py:169
  22.1 3.5 %collective-permute-start.3 = (bf16[64,3072]{1,0:T(8,128)(2,1)S(1)}, bf16[64,3072]{1,0:T(8,128)(2,1)S(1)}, u32[]{:S(2)}, u32[]{:S(2)}) collective-permute-start(bf16[64,3072]{1,0:T(8,128)(2,1)S(1)} %shard_map.56), channel_id=1, source_target_pairs={{0,8},{4,12},{8,0},{12,4},{1,9},{5,13},{9,1},{13,5},{2,10},{6,14},... | collective-permute-start | bytes 1179656 | tf_op jit(solution)/shard_map/ppermute | solution.py:169
  25.6 4.7 %collective-permute-start.1 = (bf16[64,3072]{1,0:T(8,128)(2,1)S(1)}, bf16[64,3072]{1,0:T(8,128)(2,1)S(1)}, u32[]{:S(2)}, u32[]{:S(2)}) collective-permute-start(bf16[64,3072]{1,0:T(8,128)(2,1)S(1)} %shard_map.55), channel_id=1, source_target_pairs={{0,2},{2,0},{1,3},{3,1},{4,6},{6,4},{5,7},{7,5},{8,10},{10,8},{9,1... | collective-permute-start | bytes 1179656 | tf_op jit(solution)/shard_map/ppermute | solution.py:189
  30.3 8.9 %collective-permute-done.3 = bf16[64,3072]{1,0:T(8,128)(2,1)S(1)} collective-permute-done((bf16[64,3072]{1,0:T(8,128)(2,1)S(1)}, bf16[64,3072]{1,0:T(8,128)(2,1)S(1)}, u32[]{:S(2)}, u32[]{:S(2)}) %collective-permute-start.3) | collective-permute-done | bytes 393248 | tf_op jit(solution)/shard_map/ppermute | solution.py:169
  39.4 4.7 %collective-permute-start.8 = (bf16[4,64,3072]{2,1,0:T(8,128)(2,1)S(1)}, bf16[4,64,3072]{2,1,0:T(8,128)(2,1)}, u32[]{:S(2)}, u32[]{:S(2)}) collective-permute-start(bf16[4,64,3072]{2,1,0:T(8,128)(2,1)S(1)} %shard_map.57.refs_1_.refs_4_), channel_id=1, source_target_pairs={{0,2},{2,0},{1,3},{3,1},{4,6},{6,4},{5,7},{7,5},{8,10},{10,8},{9,1... | collective-permute-start | bytes 4718600 | tf_op jit(solution)/shard_map/ppermute | solution.py:191
  44.8 6.2 %collective-permute-start.9 = (bf16[2,64,3072]{2,1,0:T(8,128)(2,1)S(1)}, bf16[2,64,3072]{2,1,0:T(8,128)(2,1)S(1)}, u32[]{:S(2)}, u32[]{:S(2)}) collective-permute-start(bf16[2,64,3072]{2,1,0:T(8,128)(2,1)S(1)} %shard_map.58.refs_0_), channel_id=1, source_target_pairs={{0,1},{1,0},{2,3},{3,2},{4,5},{5,4},{6,7},{7,6},{8,9},{9,8},{10,11... | collective-permute-start | bytes 2359304 | tf_op jit(solution)/shard_map/ppermute | solution.py:195
  51.0 1.9 %collective-permute-start.5 = (bf16[2,64,3072]{2,1,0:T(8,128)(2,1)S(1)}, bf16[2,64,3072]{2,1,0:T(8,128)(2,1)}, u32[]{:S(2)}, u32[]{:S(2)}) collective-permute-start(bf16[2,64,3072]{2,1,0:T(8,128)(2,1)S(1)} %shard_map.58.refs_0_), channel_id=1, source_target_pairs={{0,4},{4,8},{8,12},{12,0},{1,5},{5,9},{9,13},{13,1},{2,6},{6,10},{... | collective-permute-start | bytes 2359304 | tf_op jit(solution)/shard_map/ppermute | solution.py:169
  53.0 2.4 %collective-permute-start.6 = (bf16[2,64,3072]{2,1,0:T(8,128)(2,1)S(1)}, bf16[2,64,3072]{2,1,0:T(8,128)(2,1)}, u32[]{:S(2)}, u32[]{:S(2)}) collective-permute-start(bf16[2,64,3072]{2,1,0:T(8,128)(2,1)S(1)} %shard_map.58.refs_0_), channel_id=1, source_target_pairs={{0,8},{4,12},{8,0},{12,4},{1,9},{5,13},{9,1},{13,5},{2,10},{6,14},... | collective-permute-start | bytes 2359304 | tf_op jit(solution)/shard_map/ppermute | solution.py:169
  55.3 4.1 %collective-permute-start.7 = (bf16[2,64,3072]{2,1,0:T(8,128)(2,1)S(1)}, bf16[2,64,3072]{2,1,0:T(8,128)(2,1)}, u32[]{:S(2)}, u32[]{:S(2)}) collective-permute-start(bf16[2,64,3072]{2,1,0:T(8,128)(2,1)S(1)} %shard_map.58.refs_0_), channel_id=1, source_target_pairs={{0,12},{4,0},{8,4},{12,8},{1,13},{5,1},{9,5},{13,9},{2,14},{6,2},{... | collective-permute-start | bytes 2359304 | tf_op jit(solution)/shard_map/ppermute | solution.py:169
  60.2 5.4 %all-to-all-start = ((s32[16,1,128]{2,1,0:T(1,128)}), s32[16,1,128]{2,1,0:T(1,128)S(1)}, u32[]{:S(2)}, u32[]{:S(2)}) async-start(s32[16,1,128]{2,1,0:T(1,128)} %bitcast.12), calls=%async_computation | async-start | bytes 16384 | tf_op jit(solution)/shard_map/all_to_all | solution.py:197
  65.5 2.0 %collective-permute-start.13 = (bf16[4,64,3072]{2,1,0:T(8,128)(2,1)S(1)}, bf16[4,64,3072]{2,1,0:T(8,128)(2,1)}, u32[]{:S(2)}, u32[]{:S(2)}) collective-permute-start(bf16[4,64,3072]{2,1,0:T(8,128)(2,1)S(1)} %shard_map.57.refs_1_.refs_4_), channel_id=1, source_target_pairs={{0,1},{1,0},{2,3},{3,2},{4,5},{5,4},{6,7},{7,6},{8,9},{9,8},{10,11... | collective-permute-start | bytes 4718600 | tf_op jit(solution)/shard_map/ppermute | solution.py:201
  67.5 25.7 %all-to-all-done = s32[16,1,128]{2,1,0:T(1,128)S(1)} async-done(((s32[16,1,128]{2,1,0:T(1,128)}), s32[16,1,128]{2,1,0:T(1,128)S(1)}, u32[]{:S(2)}, u32[]{:S(2)}) %all-to-all-start) | async-done | bytes 8224 | tf_op jit(solution)/shard_map/all_to_all | solution.py:197
  93.3 2.3 %collective-permute-start.14 = (bf16[4,64,3072]{2,1,0:T(8,128)(2,1)}, bf16[4,64,3072]{2,1,0:T(8,128)(2,1)}, u32[]{:S(2)}, u32[]{:S(2)}) collective-permute-start(bf16[4,64,3072]{2,1,0:T(8,128)(2,1)} %shard_map.60.refs_5_), channel_id=1, source_target_pairs={{0,1},{1,0},{2,3},{3,2},{4,5},{5,4},{6,7},{7,6},{8,9},{9,8},{10,11... | collective-permute-start | bytes 4718600 | tf_op jit(solution)/shard_map/ppermute | solution.py:201
  95.6 2.0 %collective-permute-start.10 = (bf16[2,64,3072]{2,1,0:T(8,128)(2,1)}, bf16[2,64,3072]{2,1,0:T(8,128)(2,1)S(1)}, u32[]{:S(2)}, u32[]{:S(2)}) collective-permute-start(bf16[2,64,3072]{2,1,0:T(8,128)(2,1)} %collective-permute-done.5.refs_1_), channel_id=1, source_target_pairs={{0,1},{1,0},{2,3},{3,2},{4,5},{5,4},{6,7},{7,6},{8,9},{9,8},{10,11... | collective-permute-start | bytes 2359304 | tf_op jit(solution)/shard_map/ppermute | solution.py:201
  97.6 2.3 %collective-permute-start.11 = (bf16[2,64,3072]{2,1,0:T(8,128)(2,1)}, bf16[2,64,3072]{2,1,0:T(8,128)(2,1)S(1)}, u32[]{:S(2)}, u32[]{:S(2)}) collective-permute-start(bf16[2,64,3072]{2,1,0:T(8,128)(2,1)} %collective-permute-done.6.refs_2_), channel_id=1, source_target_pairs={{0,1},{1,0},{2,3},{3,2},{4,5},{5,4},{6,7},{7,6},{8,9},{9,8},{10,11... | collective-permute-start | bytes 2359304 | tf_op jit(solution)/shard_map/ppermute | solution.py:201
  100.0 2.2 %collective-permute-start.12 = (bf16[2,64,3072]{2,1,0:T(8,128)(2,1)}, bf16[2,64,3072]{2,1,0:T(8,128)(2,1)S(1)}, u32[]{:S(2)}, u32[]{:S(2)}) collective-permute-start(bf16[2,64,3072]{2,1,0:T(8,128)(2,1)} %collective-permute-done.7.refs_3_), channel_id=1, source_target_pairs={{0,1},{1,0},{2,3},{3,2},{4,5},{5,4},{6,7},{7,6},{8,9},{9,8},{10,11... | collective-permute-start | bytes 2359304 | tf_op jit(solution)/shard_map/ppermute | solution.py:201
  102.2 3.7 %multiply_cosine_fusion = (f32[2048,64]{1,0:T(8,128)S(1)}, f32[2048,64]{1,0:T(8,128)S(1)}) fusion(f32[64]{0:T(128)S(1)} %multiply_power_fusion, f32[2048]{0:T(1024)S(1)} %convert_element_type.8), kind=kLoop, calls=%fused_computation.2 | loop fusion | flops 131072 | bytes 1057024 | tf_op jit(solution)/shard_map/cos | solution.py:133
  105.9 1.3 %pad_maximum_fusion.1.refs_15_ = f32[2048,128]{1,0:T(8,128)} fusion(f32[2048,64]{1,0:T(8,128)S(1)} %get-tuple-element.10, f32[2048,64]{1,0:T(8,128)S(1)} %get-tuple-element.9), kind=kLoop, calls=%fused_computation.3 | loop fusion | flops 262144 | bytes 2097152 | tf_op jit(solution)/shard_map/concatenate | solution.py:133
  108.6 13.5 %shard_map.61 = bf16[3,2048,128]{2,1,0:T(8,128)(2,1)} custom-call(s32[3]{0:T(128)} %copy-done.5, bf16[2,64,3072]{2,1,0:T(8,128)(2,1)} %copy-done.1, bf16[2,64,3072]{2,1,0:T(8,128)(2,1)} %collective-permute-done.5.refs_1_, bf16[2,64,3072]{2,1,0:T(8,128)(2,1)} %collective-permute-done.6.refs_2_, bf16[2,64,3072]{2,1,0:T(8,128)(2,1)} %collective-permute-done.7.refs_3_, ...), custom_call_target="tpu_custom_call" | custom-call | flops 4831838208 | bytes 16515072 | tf_op jit(solution)/shard_map/pallas_call | solution.py:143
  (53 shorter events, 3.6 us)
Async XLA Ops:
  6.5 101.6 %all-gather.2.cloned.1.call-start = ((), (), s32[]{:S(2)}) async-start(), calls=%async_computation.1 | async-start | bytes 2506752 | tf_op jit(solution)/shard_map/all_gather | solution.py:185
  6.5 5.9 %collective-permute-start = (bf16[3,96,128]{2,1,0:T(8,128)(2,1)}, bf16[3,96,128]{2,1,0:T(8,128)(2,1)S(1)}, u32[]{:S(2)}, u32[]{:S(2)}) collective-permute-start(bf16[3,96,128]{2,1,0:T(8,128)(2,1)} %bitcast.41), channel_id=1, source_target_pairs={{0,16},{16,0},{1,17},{17,1},{2,18},{18,2},{3,19},{19,3},{4,20},{20... | collective-permute-start | bytes 221192 | tf_op jit(solution)/shard_map/ppermute | solution.py:180
  14.0 1.2 copy-start.2
  15.3 15.0 %collective-permute-start.4 = (bf16[64,3072]{1,0:T(8,128)(2,1)S(1)}, bf16[64,3072]{1,0:T(8,128)(2,1)S(1)}, u32[]{:S(2)}, u32[]{:S(2)}) collective-permute-start(bf16[64,3072]{1,0:T(8,128)(2,1)S(1)} %shard_map.56), channel_id=1, source_target_pairs={{0,12},{4,0},{8,4},{12,8},{1,13},{5,1},{9,5},{13,9},{2,14},{6,2},{... | collective-permute-start | bytes 1179656 | tf_op jit(solution)/shard_map/ppermute | solution.py:169
  20.1 10.2 %collective-permute-start.2 = (bf16[64,3072]{1,0:T(8,128)(2,1)S(1)}, bf16[64,3072]{1,0:T(8,128)(2,1)S(1)}, u32[]{:S(2)}, u32[]{:S(2)}) collective-permute-start(bf16[64,3072]{1,0:T(8,128)(2,1)S(1)} %shard_map.56), channel_id=1, source_target_pairs={{0,4},{4,8},{8,12},{12,0},{1,5},{5,9},{9,13},{13,1},{2,6},{6,10},{... | collective-permute-start | bytes 1179656 | tf_op jit(solution)/shard_map/ppermute | solution.py:169
  22.1 17.1 %collective-permute-start.3 = (bf16[64,3072]{1,0:T(8,128)(2,1)S(1)}, bf16[64,3072]{1,0:T(8,128)(2,1)S(1)}, u32[]{:S(2)}, u32[]{:S(2)}) collective-permute-start(bf16[64,3072]{1,0:T(8,128)(2,1)S(1)} %shard_map.56), channel_id=1, source_target_pairs={{0,8},{4,12},{8,0},{12,4},{1,9},{5,13},{9,1},{13,5},{2,10},{6,14},... | collective-permute-start | bytes 1179656 | tf_op jit(solution)/shard_map/ppermute | solution.py:169
  25.6 13.8 %collective-permute-start.1 = (bf16[64,3072]{1,0:T(8,128)(2,1)S(1)}, bf16[64,3072]{1,0:T(8,128)(2,1)S(1)}, u32[]{:S(2)}, u32[]{:S(2)}) collective-permute-start(bf16[64,3072]{1,0:T(8,128)(2,1)S(1)} %shard_map.55), channel_id=1, source_target_pairs={{0,2},{2,0},{1,3},{3,1},{4,6},{6,4},{5,7},{7,5},{8,10},{10,8},{9,1... | collective-permute-start | bytes 1179656 | tf_op jit(solution)/shard_map/ppermute | solution.py:189
  39.4 4.7 %copy-start.6 = (bf16[3,128]{1,0:T(4,128)(2,1)S(1)}, bf16[3,128]{1,0:T(4,128)(2,1)}, u32[]{:S(2)}) copy-start(bf16[3,128]{1,0:T(4,128)(2,1)} %param.8) | copy-start | bytes 2308
  39.4 26.1 %copy-start = (bf16[4,64,3072]{2,1,0:T(8,128)(2,1)}, bf16[4,64,3072]{2,1,0:T(8,128)(2,1)S(1)}, u32[]{:S(2)}) copy-start(bf16[4,64,3072]{2,1,0:T(8,128)(2,1)S(1)} %shard_map.57.refs_1_.refs_4_) | copy-start | bytes 4718596
  39.4 53.8 %collective-permute-start.8 = (bf16[4,64,3072]{2,1,0:T(8,128)(2,1)S(1)}, bf16[4,64,3072]{2,1,0:T(8,128)(2,1)}, u32[]{:S(2)}, u32[]{:S(2)}) collective-permute-start(bf16[4,64,3072]{2,1,0:T(8,128)(2,1)S(1)} %shard_map.57.refs_1_.refs_4_), channel_id=1, source_target_pairs={{0,2},{2,0},{1,3},{3,1},{4,6},{6,4},{5,7},{7,5},{8,10},{10,8},{9,1... | collective-permute-start | bytes 4718600 | tf_op jit(solution)/shard_map/ppermute | solution.py:191
  44.3 15.2 %copy-start.7 = (s32[128]{0:T(128)S(1)}, s32[128]{0:T(128)}, u32[]{:S(2)}) copy-start(s32[128]{0:T(128)} %param.6) | copy-start | bytes 1540
  44.8 48.4 %copy-start.1 = (bf16[2,64,3072]{2,1,0:T(8,128)(2,1)}, bf16[2,64,3072]{2,1,0:T(8,128)(2,1)S(1)}, u32[]{:S(2)}) copy-start(bf16[2,64,3072]{2,1,0:T(8,128)(2,1)S(1)} %shard_map.58.refs_0_) | copy-start | bytes 2359300
  44.8 14.6 %collective-permute-start.9 = (bf16[2,64,3072]{2,1,0:T(8,128)(2,1)S(1)}, bf16[2,64,3072]{2,1,0:T(8,128)(2,1)S(1)}, u32[]{:S(2)}, u32[]{:S(2)}) collective-permute-start(bf16[2,64,3072]{2,1,0:T(8,128)(2,1)S(1)} %shard_map.58.refs_0_), channel_id=1, source_target_pairs={{0,1},{1,0},{2,3},{3,2},{4,5},{5,4},{6,7},{7,6},{8,9},{9,8},{10,11... | collective-permute-start | bytes 2359304 | tf_op jit(solution)/shard_map/ppermute | solution.py:195
  51.0 44.6 %collective-permute-start.5 = (bf16[2,64,3072]{2,1,0:T(8,128)(2,1)S(1)}, bf16[2,64,3072]{2,1,0:T(8,128)(2,1)}, u32[]{:S(2)}, u32[]{:S(2)}) collective-permute-start(bf16[2,64,3072]{2,1,0:T(8,128)(2,1)S(1)} %shard_map.58.refs_0_), channel_id=1, source_target_pairs={{0,4},{4,8},{8,12},{12,0},{1,5},{5,9},{9,13},{13,1},{2,6},{6,10},{... | collective-permute-start | bytes 2359304 | tf_op jit(solution)/shard_map/ppermute | solution.py:169
  53.0 44.7 %collective-permute-start.6 = (bf16[2,64,3072]{2,1,0:T(8,128)(2,1)S(1)}, bf16[2,64,3072]{2,1,0:T(8,128)(2,1)}, u32[]{:S(2)}, u32[]{:S(2)}) collective-permute-start(bf16[2,64,3072]{2,1,0:T(8,128)(2,1)S(1)} %shard_map.58.refs_0_), channel_id=1, source_target_pairs={{0,8},{4,12},{8,0},{12,4},{1,9},{5,13},{9,1},{13,5},{2,10},{6,14},... | collective-permute-start | bytes 2359304 | tf_op jit(solution)/shard_map/ppermute | solution.py:169
  55.3 44.6 %collective-permute-start.7 = (bf16[2,64,3072]{2,1,0:T(8,128)(2,1)S(1)}, bf16[2,64,3072]{2,1,0:T(8,128)(2,1)}, u32[]{:S(2)}, u32[]{:S(2)}) collective-permute-start(bf16[2,64,3072]{2,1,0:T(8,128)(2,1)S(1)} %shard_map.58.refs_0_), channel_id=1, source_target_pairs={{0,12},{4,0},{8,4},{12,8},{1,13},{5,1},{9,5},{13,9},{2,14},{6,2},{... | collective-permute-start | bytes 2359304 | tf_op jit(solution)/shard_map/ppermute | solution.py:169
  59.5 33.8 %copy-start.3 = (bf16[2,64,3072]{2,1,0:T(8,128)(2,1)}, bf16[2,64,3072]{2,1,0:T(8,128)(2,1)S(1)}, u32[]{:S(2)}) copy-start(bf16[2,64,3072]{2,1,0:T(8,128)(2,1)S(1)} %collective-permute-done.9.refs_1_.refs_6_) | copy-start | bytes 2359300
  60.2 33.1 %all-to-all-start = ((s32[16,1,128]{2,1,0:T(1,128)}), s32[16,1,128]{2,1,0:T(1,128)S(1)}, u32[]{:S(2)}, u32[]{:S(2)}) async-start(s32[16,1,128]{2,1,0:T(1,128)} %bitcast.12), calls=%async_computation | async-start | bytes 16384 | tf_op jit(solution)/shard_map/all_to_all | solution.py:197
  65.5 41.7 %collective-permute-start.13 = (bf16[4,64,3072]{2,1,0:T(8,128)(2,1)S(1)}, bf16[4,64,3072]{2,1,0:T(8,128)(2,1)}, u32[]{:S(2)}, u32[]{:S(2)}) collective-permute-start(bf16[4,64,3072]{2,1,0:T(8,128)(2,1)S(1)} %shard_map.57.refs_1_.refs_4_), channel_id=1, source_target_pairs={{0,1},{1,0},{2,3},{3,2},{4,5},{5,4},{6,7},{7,6},{8,9},{9,8},{10,11... | collective-permute-start | bytes 4718600 | tf_op jit(solution)/shard_map/ppermute | solution.py:201
  93.3 14.9 %collective-permute-start.14 = (bf16[4,64,3072]{2,1,0:T(8,128)(2,1)}, bf16[4,64,3072]{2,1,0:T(8,128)(2,1)}, u32[]{:S(2)}, u32[]{:S(2)}) collective-permute-start(bf16[4,64,3072]{2,1,0:T(8,128)(2,1)} %shard_map.60.refs_5_), channel_id=1, source_target_pairs={{0,1},{1,0},{2,3},{3,2},{4,5},{5,4},{6,7},{7,6},{8,9},{9,8},{10,11... | collective-permute-start | bytes 4718600 | tf_op jit(solution)/shard_map/ppermute | solution.py:201
  95.6 11.6 %collective-permute-start.10 = (bf16[2,64,3072]{2,1,0:T(8,128)(2,1)}, bf16[2,64,3072]{2,1,0:T(8,128)(2,1)S(1)}, u32[]{:S(2)}, u32[]{:S(2)}) collective-permute-start(bf16[2,64,3072]{2,1,0:T(8,128)(2,1)} %collective-permute-done.5.refs_1_), channel_id=1, source_target_pairs={{0,1},{1,0},{2,3},{3,2},{4,5},{5,4},{6,7},{7,6},{8,9},{9,8},{10,11... | collective-permute-start | bytes 2359304 | tf_op jit(solution)/shard_map/ppermute | solution.py:201
  97.6 9.6 %collective-permute-start.11 = (bf16[2,64,3072]{2,1,0:T(8,128)(2,1)}, bf16[2,64,3072]{2,1,0:T(8,128)(2,1)S(1)}, u32[]{:S(2)}, u32[]{:S(2)}) collective-permute-start(bf16[2,64,3072]{2,1,0:T(8,128)(2,1)} %collective-permute-done.6.refs_2_), channel_id=1, source_target_pairs={{0,1},{1,0},{2,3},{3,2},{4,5},{5,4},{6,7},{7,6},{8,9},{9,8},{10,11... | collective-permute-start | bytes 2359304 | tf_op jit(solution)/shard_map/ppermute | solution.py:201
  100.0 7.3 %collective-permute-start.12 = (bf16[2,64,3072]{2,1,0:T(8,128)(2,1)}, bf16[2,64,3072]{2,1,0:T(8,128)(2,1)S(1)}, u32[]{:S(2)}, u32[]{:S(2)}) collective-permute-start(bf16[2,64,3072]{2,1,0:T(8,128)(2,1)} %collective-permute-done.7.refs_3_), channel_id=1, source_target_pairs={{0,1},{1,0},{2,3},{3,2},{4,5},{5,4},{6,7},{7,6},{8,9},{9,8},{10,11... | collective-permute-start | bytes 2359304 | tf_op jit(solution)/shard_map/ppermute | solution.py:201
  107.2 1.4 %copy-start.10 = (bf16[2,64,3072]{2,1,0:T(8,128)(2,1)}, bf16[2,64,3072]{2,1,0:T(8,128)(2,1)S(1)}, u32[]{:S(2)}) copy-start(bf16[2,64,3072]{2,1,0:T(8,128)(2,1)S(1)} %collective-permute-done.12.refs_9_) | copy-start | bytes 2359300
  (4 other events, 3.2 us)
Sparse Core Ops, SparseCore 0:
  14.1 72.1 all-gather.1

commit v5 on v3

--- a/solution.py
+++ b/solution.py
@@ -19,7 +19,7 @@
     count = Y + 2
     (*near_own, far_own_ref, far_other_ref), (*near_across, x_far_own_ref, x_far_other_ref) = refs[:count], refs[count : 2 * count]
     refs = refs[2 * count :]
-    w_ref, bias_ref, taps_ref, turns_ref, out_ref, held, w_flat, turns, keys, turns_sem, out_sems, w_sems, sems = refs
+    w_ref, bias_ref, taps_ref, cos_ref, sin_ref, out_ref, held, w_flat, keys, out_sems, w_sems, sems = refs
     shards, rows, depth = held.shape
     pieces, heads = w_ref.shape[0], out_ref.shape[0]
     piece_rows = w_ref.shape[1] // heads
@@ -65,17 +65,14 @@
             for copy in copies_of(y, 0, 0):
                 copy.wait()
 
-    load_turns = pltpu.make_async_copy(turns_ref, turns, turns_sem)
     for load in loads:
         load.start()
     start_block(0)
-    load_turns.start()
     for load in loads:
         load.wait()
 
     block_rows = BATCH * rows
     row = lax.broadcasted_iota(jnp.int32, (block_rows, HEAD_DIM), 0)
-    is_first = lax.broadcasted_iota(jnp.int32, (block_rows, HEAD_DIM), 1) < HEAD_DIM // 2
     stores = []
     tail = None
     for first in range(0, shards, BATCH):
@@ -87,12 +84,10 @@
         projected = jnp.dot(block, w_flat[...], preferred_element_type=jnp.float32) + bias_ref[...]
         if start % SEQ_LEN == 0:
             tail = jnp.zeros((8, projected.shape[1]), jnp.float32)
-        if first == 0:
-            load_turns.wait()
-        turn = turns[start : start + block_rows, :]
-        other_turn = pltpu.roll(turn, HEAD_DIM // 2, 1)
-        cosine = jnp.where(is_first, turn, other_turn)
-        sine = jnp.where(is_first, -other_turn, turn)
+        half_cosine = cos_ref[start : start + block_rows, :]
+        half_sine = sin_ref[start : start + block_rows, :]
+        cosine = jnp.concatenate([half_cosine, half_cosine], axis=1)
+        sine = jnp.concatenate([-half_sine, half_sine], axis=1)
         for head in range(heads):
             lanes = slice(head * HEAD_DIM, (head + 1) * HEAD_DIM)
             now = projected[:, lanes]
@@ -130,10 +125,10 @@
     half_dim = HEAD_DIM // 2
     inv_freq = rope_base ** (-(jnp.arange(half_dim, dtype=jnp.float32) * 2.0) / HEAD_DIM)
     angles = places.astype(jnp.float32)[:, None] * inv_freq[None, :]
-    return jnp.concatenate([jnp.cos(angles), jnp.sin(angles)], axis=1)
-
-
-def keys_of(where, gathered, weight, bias, taps, turns):
+    return jnp.cos(angles), jnp.sin(angles)
+
+
+def keys_of(where, gathered, weight, bias, taps, *turns):
     rows, depth = gathered[0].shape[1] + gathered[Y].shape[1], gathered[0].shape[2]
     shards = Y * X_HI * CORE
     columns = bias.shape[1]
@@ -142,15 +137,13 @@
     vmem, any_space = pl.BlockSpec(memory_space=pltpu.VMEM), pl.BlockSpec(memory_space=pl.ANY)
     return pl.pallas_call(
         keys_kernel,
-        in_specs=[pl.BlockSpec(memory_space=pltpu.SMEM)] + [any_space] * (len(gathered) + 1) + [vmem] * 2 + [any_space],
+        in_specs=[pl.BlockSpec(memory_space=pltpu.SMEM)] + [any_space] * (len(gathered) + 1) + [vmem] * 4,
         out_specs=any_space,
         out_shape=jax.ShapeDtypeStruct((heads, total, HEAD_DIM), jnp.bfloat16),
         scratch_shapes=[
             pltpu.VMEM((shards, rows, depth), jnp.bfloat16),
             pltpu.VMEM((depth, columns), jnp.bfloat16),
-            pltpu.VMEM((total, HEAD_DIM), jnp.float32),
             pltpu.VMEM((heads, total, HEAD_DIM), jnp.bfloat16),
-            pltpu.SemaphoreType.DMA,
             pltpu.SemaphoreType.DMA((shards // BATCH,)),
             pltpu.SemaphoreType.DMA((weight.shape[0] * heads,)),
             pltpu.SemaphoreType.DMA((2 * shards,)),
@@ -161,7 +154,7 @@
             bytes_accessed=2 * (total * depth + depth * columns + total * columns),
             transcendentals=0,
         ),
-    )(where, *gathered, weight, bias, taps, turns)
+    )(where, *gathered, weight, bias, taps, *turns)
 
 
 def along_y(value):
@@ -199,7 +192,7 @@
     gathered += tuple(lax.ppermute(piece, "core", across) for piece in gathered)
 
     taps = jnp.transpose(conv_taps, (1, 0, 2)).reshape(conv_taps.shape[1], columns)
-    keys = keys_of(where, gathered, weight, bias, taps, turns)
+    keys = keys_of(where, gathered, weight, bias, taps, *turns)
     return jnp.transpose(keys, (1, 0, 2))
 
 

time: 124 us -> 134 us (1.081)
  waiting for transfers between devices: 34.2 us -> 44.5 us
    all_to_all x1, waiting for transfers between devices: 0.39 us -> 6.96 us  [body(): lax.all_to_all(sent, ('y', 'x_hi', 'core'), 0, 0, tiled=True).reshape(-1)]
    sin x0 -> x1, other arithmetic: none -> 5.61 us  [rotation(): return (jnp.cos(angles), jnp.sin(angles))]
    cos x1 -> x0, other arithmetic: 3.68 us -> none  [rotation(): return jnp.concatenate([jnp.cos(angles), jnp.sin(angles)], axis=1)]
    ppermute x6, waiting for transfers between devices: 11.1 us -> 14.7 us  [step(): return lax.ppermute(value, 'y', [(i, (i + k) % Y) for i in range(Y)])]
    all_to_all x1, starting transfers between devices: 4.71 us -> 3.32 us  [body(): lax.all_to_all(sent, ('y', 'x_hi', 'core'), 0, 0, tiled=True).reshape(-1)]
  transfers between devices with their start and end apart: 17 -> 17, of which waited for: 5 -> 6; matrix products, arithmetic and copies ran while one was open for 6% -> 6% of each run, Pallas kernels for 0% -> 0%
where the time goes in v5:
time: 134 us; the launch traced here: 133 us
  starting transfers between devices  51.1 us (38%)
  waiting for transfers between devices  44.5 us (33%)
  Pallas kernels  14.1 us (11%)
  between operations  13.8 us (10%)
  other arithmetic  7.56 us (6%)
  local copies, waits for them, and re-layouts  2.23 us (2%)
    ppermute x1, waiting for transfers between devices, body(): far_other = lax.ppermute(far_own, 'x_hi', across)  20.8 us
    ppermute x6, starting transfers between devices, step(): return lax.ppermute(value, 'y', [(i, (i + k) % Y) for i in range(Y)])  16.9 us
    ppermute x6, starting transfers between devices, body(): lax.ppermute(piece, 'core', across)  15.3 us
    ppermute x6, waiting for transfers between devices, step(): return lax.ppermute(value, 'y', [(i, (i + k) % Y) for i in range(Y)])  14.7 us
    pallas_call x1, Pallas kernels, keys_of(): pl.pallas_call(keys_kernel, in_specs=[pl.BlockSpec(memory_space=pltpu.SME...  14.1 us
    all_to_all x1, waiting for transfers between devices, body(): lax.all_to_all(sent, ('y', 'x_hi', 'core'), 0, 0, tiled=True).reshape(-1)  6.96 us
    ppermute x1, starting transfers between devices, body(): far_other = lax.ppermute(far_own, 'x_hi', across)  6.92 us
    sin x1, other arithmetic, rotation(): return (jnp.cos(angles), jnp.sin(angles))  5.61 us
  transfers between devices with their start and end apart: 17, of which 6 were waited for; matrix products, arithmetic and copies ran while one was open for 6% of the time, Pallas kernels for 0%

profile of v5, /device:TPU:1, one launch (start us, length us, event | category | flops | bytes accessed | tf_op | source)
XLA Modules:
  0.0 133.3 jit_solution(16822967615718977865)
XLA Ops:
  6.5 3.9 %collective-permute-start = (bf16[3,96,128]{2,1,0:T(8,128)(2,1)}, bf16[3,96,128]{2,1,0:T(8,128)(2,1)S(1)}, u32[]{:S(2)}, u32[]{:S(2)}) collective-permute-start(bf16[3,96,128]{2,1,0:T(8,128)(2,1)} %bitcast.36), channel_id=1, source_target_pairs={{0,16},{16,0},{1,17},{17,1},{2,18},{18,2},{3,19},{19,3},{4,20},{20... | collective-permute-start | bytes 221192 | tf_op jit(solution)/shard_map/ppermute | solution.py:173
  10.5 1.9 %collective-permute-done = bf16[3,96,128]{2,1,0:T(8,128)(2,1)S(1)} collective-permute-done((bf16[3,96,128]{2,1,0:T(8,128)(2,1)}, bf16[3,96,128]{2,1,0:T(8,128)(2,1)S(1)}, u32[]{:S(2)}, u32[]{:S(2)}) %collective-permute-start) | collective-permute-done | bytes 73760 | tf_op jit(solution)/shard_map/ppermute | solution.py:173
  14.0 1.2 fusion
  15.3 4.9 %collective-permute-start.4 = (bf16[64,3072]{1,0:T(8,128)(2,1)S(1)}, bf16[64,3072]{1,0:T(8,128)(2,1)S(1)}, u32[]{:S(2)}, u32[]{:S(2)}) collective-permute-start(bf16[64,3072]{1,0:T(8,128)(2,1)S(1)} %shard_map.56), channel_id=1, source_target_pairs={{0,12},{4,0},{8,4},{12,8},{1,13},{5,1},{9,5},{13,9},{2,14},{6,2},{... | collective-permute-start | bytes 1179656 | tf_op jit(solution)/shard_map/ppermute | solution.py:162
  20.1 2.3 %collective-permute-start.3 = (bf16[64,3072]{1,0:T(8,128)(2,1)S(1)}, bf16[64,3072]{1,0:T(8,128)(2,1)S(1)}, u32[]{:S(2)}, u32[]{:S(2)}) collective-permute-start(bf16[64,3072]{1,0:T(8,128)(2,1)S(1)} %shard_map.56), channel_id=1, source_target_pairs={{0,8},{4,12},{8,0},{12,4},{1,9},{5,13},{9,1},{13,5},{2,10},{6,14},... | collective-permute-start | bytes 1179656 | tf_op jit(solution)/shard_map/ppermute | solution.py:162
  22.4 2.6 %collective-permute-start.2 = (bf16[64,3072]{1,0:T(8,128)(2,1)S(1)}, bf16[64,3072]{1,0:T(8,128)(2,1)S(1)}, u32[]{:S(2)}, u32[]{:S(2)}) collective-permute-start(bf16[64,3072]{1,0:T(8,128)(2,1)S(1)} %shard_map.56), channel_id=1, source_target_pairs={{0,4},{4,8},{8,12},{12,0},{1,5},{5,9},{9,13},{13,1},{2,6},{6,10},{... | collective-permute-start | bytes 1179656 | tf_op jit(solution)/shard_map/ppermute | solution.py:162
  25.0 4.7 %collective-permute-start.1 = (bf16[64,3072]{1,0:T(8,128)(2,1)S(1)}, bf16[64,3072]{1,0:T(8,128)(2,1)S(1)}, u32[]{:S(2)}, u32[]{:S(2)}) collective-permute-start(bf16[64,3072]{1,0:T(8,128)(2,1)S(1)} %shard_map.55), channel_id=1, source_target_pairs={{0,2},{2,0},{1,3},{3,1},{4,6},{6,4},{5,7},{7,5},{8,10},{10,8},{9,1... | collective-permute-start | bytes 1179656 | tf_op jit(solution)/shard_map/ppermute | solution.py:182
  30.4 10.3 %collective-permute-done.2 = bf16[64,3072]{1,0:T(8,128)(2,1)S(1)} collective-permute-done((bf16[64,3072]{1,0:T(8,128)(2,1)S(1)}, bf16[64,3072]{1,0:T(8,128)(2,1)S(1)}, u32[]{:S(2)}, u32[]{:S(2)}) %collective-permute-start.2) | collective-permute-done | bytes 393248 | tf_op jit(solution)/shard_map/ppermute | solution.py:162
  41.0 6.9 %collective-permute-start.8 = (bf16[4,64,3072]{2,1,0:T(8,128)(2,1)S(1)}, bf16[4,64,3072]{2,1,0:T(8,128)(2,1)}, u32[]{:S(2)}, u32[]{:S(2)}) collective-permute-start(bf16[4,64,3072]{2,1,0:T(8,128)(2,1)S(1)} %shard_map.57.refs_1_.refs_4_), channel_id=1, source_target_pairs={{0,2},{2,0},{1,3},{3,1},{4,6},{6,4},{5,7},{7,5},{8,10},{10,8},{9,1... | collective-permute-start | bytes 4718600 | tf_op jit(solution)/shard_map/ppermute | solution.py:186
  48.5 2.7 %collective-permute-start.9 = (bf16[2,64,3072]{2,1,0:T(8,128)(2,1)S(1)}, bf16[2,64,3072]{2,1,0:T(8,128)(2,1)S(1)}, u32[]{:S(2)}, u32[]{:S(2)}) collective-permute-start(bf16[2,64,3072]{2,1,0:T(8,128)(2,1)S(1)} %shard_map.58.refs_0_), channel_id=1, source_target_pairs={{0,1},{1,0},{2,3},{3,2},{4,5},{5,4},{6,7},{7,6},{8,9},{9,8},{10,11... | collective-permute-start | bytes 2359304 | tf_op jit(solution)/shard_map/ppermute | solution.py:192
  51.2 2.2 %collective-permute-start.7 = (bf16[2,64,3072]{2,1,0:T(8,128)(2,1)S(1)}, bf16[2,64,3072]{2,1,0:T(8,128)(2,1)}, u32[]{:S(2)}, u32[]{:S(2)}) collective-permute-start(bf16[2,64,3072]{2,1,0:T(8,128)(2,1)S(1)} %shard_map.58.refs_0_), channel_id=1, source_target_pairs={{0,12},{4,0},{8,4},{12,8},{1,13},{5,1},{9,5},{13,9},{2,14},{6,2},{... | collective-permute-start | bytes 2359304 | tf_op jit(solution)/shard_map/ppermute | solution.py:162
  53.4 2.3 %collective-permute-start.6 = (bf16[2,64,3072]{2,1,0:T(8,128)(2,1)S(1)}, bf16[2,64,3072]{2,1,0:T(8,128)(2,1)}, u32[]{:S(2)}, u32[]{:S(2)}) collective-permute-start(bf16[2,64,3072]{2,1,0:T(8,128)(2,1)S(1)} %shard_map.58.refs_0_), channel_id=1, source_target_pairs={{0,8},{4,12},{8,0},{12,4},{1,9},{5,13},{9,1},{13,5},{2,10},{6,14},... | collective-permute-start | bytes 2359304 | tf_op jit(solution)/shard_map/ppermute | solution.py:162
  55.7 2.7 %collective-permute-start.5 = (bf16[2,64,3072]{2,1,0:T(8,128)(2,1)S(1)}, bf16[2,64,3072]{2,1,0:T(8,128)(2,1)}, u32[]{:S(2)}, u32[]{:S(2)}) collective-permute-start(bf16[2,64,3072]{2,1,0:T(8,128)(2,1)S(1)} %shard_map.58.refs_0_), channel_id=1, source_target_pairs={{0,4},{4,8},{8,12},{12,0},{1,5},{5,9},{9,13},{13,1},{2,6},{6,10},{... | collective-permute-start | bytes 2359304 | tf_op jit(solution)/shard_map/ppermute | solution.py:162
  58.5 2.5 %collective-permute-start.13 = (bf16[4,64,3072]{2,1,0:T(8,128)(2,1)S(1)}, bf16[4,64,3072]{2,1,0:T(8,128)(2,1)}, u32[]{:S(2)}, u32[]{:S(2)}) collective-permute-start(bf16[4,64,3072]{2,1,0:T(8,128)(2,1)S(1)} %shard_map.57.refs_1_.refs_4_), channel_id=1, source_target_pairs={{0,1},{1,0},{2,3},{3,2},{4,5},{5,4},{6,7},{7,6},{8,9},{9,8},{10,11... | collective-permute-start | bytes 4718600 | tf_op jit(solution)/shard_map/ppermute | solution.py:192
  61.0 20.8 %collective-permute-done.8.refs_5_ = bf16[4,64,3072]{2,1,0:T(8,128)(2,1)} collective-permute-done((bf16[4,64,3072]{2,1,0:T(8,128)(2,1)S(1)}, bf16[4,64,3072]{2,1,0:T(8,128)(2,1)}, u32[]{:S(2)}, u32[]{:S(2)}) %collective-permute-start.8) | collective-permute-done | bytes 1572896 | tf_op jit(solution)/shard_map/ppermute | solution.py:186
  81.8 3.5 %collective-permute-start.14 = (bf16[4,64,3072]{2,1,0:T(8,128)(2,1)}, bf16[4,64,3072]{2,1,0:T(8,128)(2,1)}, u32[]{:S(2)}, u32[]{:S(2)}) collective-permute-start(bf16[4,64,3072]{2,1,0:T(8,128)(2,1)} %collective-permute-done.8.refs_5_), channel_id=1, source_target_pairs={{0,1},{1,0},{2,3},{3,2},{4,5},{5,4},{6,7},{7,6},{8,9},{9,8},{10,11... | collective-permute-start | bytes 4718600 | tf_op jit(solution)/shard_map/ppermute | solution.py:192
  85.3 1.9 %collective-permute-start.12 = (bf16[2,64,3072]{2,1,0:T(8,128)(2,1)}, bf16[2,64,3072]{2,1,0:T(8,128)(2,1)}, u32[]{:S(2)}, u32[]{:S(2)}) collective-permute-start(bf16[2,64,3072]{2,1,0:T(8,128)(2,1)} %collective-permute-done.7.refs_3_), channel_id=1, source_target_pairs={{0,1},{1,0},{2,3},{3,2},{4,5},{5,4},{6,7},{7,6},{8,9},{9,8},{10,11... | collective-permute-start | bytes 2359304 | tf_op jit(solution)/shard_map/ppermute | solution.py:192
  87.2 2.4 %collective-permute-start.11 = (bf16[2,64,3072]{2,1,0:T(8,128)(2,1)}, bf16[2,64,3072]{2,1,0:T(8,128)(2,1)}, u32[]{:S(2)}, u32[]{:S(2)}) collective-permute-start(bf16[2,64,3072]{2,1,0:T(8,128)(2,1)} %collective-permute-done.6.refs_2_), channel_id=1, source_target_pairs={{0,1},{1,0},{2,3},{3,2},{4,5},{5,4},{6,7},{7,6},{8,9},{9,8},{10,11... | collective-permute-start | bytes 2359304 | tf_op jit(solution)/shard_map/ppermute | solution.py:192
  89.6 3.7 %collective-permute-done.5.refs_1_ = bf16[2,64,3072]{2,1,0:T(8,128)(2,1)} collective-permute-done((bf16[2,64,3072]{2,1,0:T(8,128)(2,1)S(1)}, bf16[2,64,3072]{2,1,0:T(8,128)(2,1)}, u32[]{:S(2)}, u32[]{:S(2)}) %collective-permute-start.5) | collective-permute-done | bytes 786464 | tf_op jit(solution)/shard_map/ppermute | solution.py:162
  93.3 2.4 %collective-permute-start.10 = (bf16[2,64,3072]{2,1,0:T(8,128)(2,1)}, bf16[2,64,3072]{2,1,0:T(8,128)(2,1)}, u32[]{:S(2)}, u32[]{:S(2)}) collective-permute-start(bf16[2,64,3072]{2,1,0:T(8,128)(2,1)} %collective-permute-done.5.refs_1_), channel_id=1, source_target_pairs={{0,1},{1,0},{2,3},{3,2},{4,5},{5,4},{6,7},{7,6},{8,9},{9,8},{10,11... | collective-permute-start | bytes 2359304 | tf_op jit(solution)/shard_map/ppermute | solution.py:192
  96.3 3.3 %all-to-all-start = ((s32[16,1,128]{2,1,0:T(1,128)}), s32[16,1,128]{2,1,0:T(1,128)S(1)}, u32[]{:S(2)}, u32[]{:S(2)}) async-start(s32[16,1,128]{2,1,0:T(1,128)} %broadcast_in_dim.2), calls=%async_computation | async-start | bytes 16384 | tf_op jit(solution)/shard_map/all_to_all | solution.py:184
  99.6 7.0 %all-to-all-done = s32[16,1,128]{2,1,0:T(1,128)S(1)} async-done(((s32[16,1,128]{2,1,0:T(1,128)}), s32[16,1,128]{2,1,0:T(1,128)S(1)}, u32[]{:S(2)}, u32[]{:S(2)}) %all-to-all-start) | async-done | bytes 8224 | tf_op jit(solution)/shard_map/all_to_all | solution.py:184
  106.6 5.6 %multiply_sine_fusion = (f32[2048,64]{1,0:T(8,128)}, f32[2048,64]{1,0:T(8,128)}) fusion(f32[64]{0:T(128)S(1)} %multiply_power_fusion, f32[2048]{0:T(1024)S(1)} %bitcast.37), kind=kLoop, calls=%fused_computation.1 | loop fusion | flops 131072 | bytes 1057024 | tf_op jit(solution)/shard_map/sin | solution.py:128
  112.3 14.1 %shard_map.59 = bf16[3,2048,128]{2,1,0:T(8,128)(2,1)} custom-call(s32[3]{0:T(128)} %copy-done.4, bf16[2,64,3072]{2,1,0:T(8,128)(2,1)} %copy-done.1, bf16[2,64,3072]{2,1,0:T(8,128)(2,1)} %collective-permute-done.5.refs_1_, bf16[2,64,3072]{2,1,0:T(8,128)(2,1)} %collective-permute-done.6.refs_2_, bf16[2,64,3072]{2,1,0:T(8,128)(2,1)} %collective-permute-done.7.refs_3_, ...), custom_call_target="tpu_custom_call" | custom-call | flops 4831838208 | bytes 16515072 | tf_op jit(solution)/shard_map/pallas_call | solution.py:138
  (44 shorter events, 3.8 us)
Async XLA Ops:
  6.5 105.7 %all-gather.2.cloned.1.call-start = ((), (), s32[]{:S(2)}) async-start(), calls=%async_computation.1 | async-start | bytes 2506752 | tf_op jit(solution)/shard_map/all_gather | solution.py:178
  6.5 5.9 %collective-permute-start = (bf16[3,96,128]{2,1,0:T(8,128)(2,1)}, bf16[3,96,128]{2,1,0:T(8,128)(2,1)S(1)}, u32[]{:S(2)}, u32[]{:S(2)}) collective-permute-start(bf16[3,96,128]{2,1,0:T(8,128)(2,1)} %bitcast.36), channel_id=1, source_target_pairs={{0,16},{16,0},{1,17},{17,1},{2,18},{18,2},{3,19},{19,3},{4,20},{20... | collective-permute-start | bytes 221192 | tf_op jit(solution)/shard_map/ppermute | solution.py:173
  14.0 1.2 copy-start.2
  15.3 15.2 %collective-permute-start.4 = (bf16[64,3072]{1,0:T(8,128)(2,1)S(1)}, bf16[64,3072]{1,0:T(8,128)(2,1)S(1)}, u32[]{:S(2)}, u32[]{:S(2)}) collective-permute-start(bf16[64,3072]{1,0:T(8,128)(2,1)S(1)} %shard_map.56), channel_id=1, source_target_pairs={{0,12},{4,0},{8,4},{12,8},{1,13},{5,1},{9,5},{13,9},{2,14},{6,2},{... | collective-permute-start | bytes 1179656 | tf_op jit(solution)/shard_map/ppermute | solution.py:162
  20.1 10.3 %collective-permute-start.3 = (bf16[64,3072]{1,0:T(8,128)(2,1)S(1)}, bf16[64,3072]{1,0:T(8,128)(2,1)S(1)}, u32[]{:S(2)}, u32[]{:S(2)}) collective-permute-start(bf16[64,3072]{1,0:T(8,128)(2,1)S(1)} %shard_map.56), channel_id=1, source_target_pairs={{0,8},{4,12},{8,0},{12,4},{1,9},{5,13},{9,1},{13,5},{2,10},{6,14},... | collective-permute-start | bytes 1179656 | tf_op jit(solution)/shard_map/ppermute | solution.py:162
  22.4 18.3 %collective-permute-start.2 = (bf16[64,3072]{1,0:T(8,128)(2,1)S(1)}, bf16[64,3072]{1,0:T(8,128)(2,1)S(1)}, u32[]{:S(2)}, u32[]{:S(2)}) collective-permute-start(bf16[64,3072]{1,0:T(8,128)(2,1)S(1)} %shard_map.56), channel_id=1, source_target_pairs={{0,4},{4,8},{8,12},{12,0},{1,5},{5,9},{9,13},{13,1},{2,6},{6,10},{... | collective-permute-start | bytes 1179656 | tf_op jit(solution)/shard_map/ppermute | solution.py:162
  25.0 15.9 %collective-permute-start.1 = (bf16[64,3072]{1,0:T(8,128)(2,1)S(1)}, bf16[64,3072]{1,0:T(8,128)(2,1)S(1)}, u32[]{:S(2)}, u32[]{:S(2)}) collective-permute-start(bf16[64,3072]{1,0:T(8,128)(2,1)S(1)} %shard_map.55), channel_id=1, source_target_pairs={{0,2},{2,0},{1,3},{3,1},{4,6},{6,4},{5,7},{7,5},{8,10},{10,8},{9,1... | collective-permute-start | bytes 1179656 | tf_op jit(solution)/shard_map/ppermute | solution.py:182
  40.9 7.0 %copy-start.6 = (bf16[3,128]{1,0:T(4,128)(2,1)S(1)}, bf16[3,128]{1,0:T(4,128)(2,1)}, u32[]{:S(2)}) copy-start(bf16[3,128]{1,0:T(4,128)(2,1)} %param.8) | copy-start | bytes 2308
  41.0 17.5 %copy-start = (bf16[4,64,3072]{2,1,0:T(8,128)(2,1)}, bf16[4,64,3072]{2,1,0:T(8,128)(2,1)S(1)}, u32[]{:S(2)}) copy-start(bf16[4,64,3072]{2,1,0:T(8,128)(2,1)S(1)} %shard_map.57.refs_1_.refs_4_) | copy-start | bytes 4718596
  41.0 40.8 %collective-permute-start.8 = (bf16[4,64,3072]{2,1,0:T(8,128)(2,1)S(1)}, bf16[4,64,3072]{2,1,0:T(8,128)(2,1)}, u32[]{:S(2)}, u32[]{:S(2)}) collective-permute-start(bf16[4,64,3072]{2,1,0:T(8,128)(2,1)S(1)} %shard_map.57.refs_1_.refs_4_), channel_id=1, source_target_pairs={{0,2},{2,0},{1,3},{3,1},{4,6},{6,4},{5,7},{7,5},{8,10},{10,8},{9,1... | collective-permute-start | bytes 4718600 | tf_op jit(solution)/shard_map/ppermute | solution.py:186
  47.9 0.6 copy-start.3
  48.1 47.5 %copy-start.7 = (s32[128]{0:T(128)S(1)}, s32[128]{0:T(128)}, u32[]{:S(2)}) copy-start(s32[128]{0:T(128)} %param.6) | copy-start | bytes 1540
  48.5 63.7 %copy-start.1 = (bf16[2,64,3072]{2,1,0:T(8,128)(2,1)}, bf16[2,64,3072]{2,1,0:T(8,128)(2,1)S(1)}, u32[]{:S(2)}) copy-start(bf16[2,64,3072]{2,1,0:T(8,128)(2,1)S(1)} %shard_map.58.refs_0_) | copy-start | bytes 2359300
  48.5 9.9 %collective-permute-start.9 = (bf16[2,64,3072]{2,1,0:T(8,128)(2,1)S(1)}, bf16[2,64,3072]{2,1,0:T(8,128)(2,1)S(1)}, u32[]{:S(2)}, u32[]{:S(2)}) collective-permute-start(bf16[2,64,3072]{2,1,0:T(8,128)(2,1)S(1)} %shard_map.58.refs_0_), channel_id=1, source_target_pairs={{0,1},{1,0},{2,3},{3,2},{4,5},{5,4},{6,7},{7,6},{8,9},{9,8},{10,11... | collective-permute-start | bytes 2359304 | tf_op jit(solution)/shard_map/ppermute | solution.py:192
  51.2 34.1 %collective-permute-start.7 = (bf16[2,64,3072]{2,1,0:T(8,128)(2,1)S(1)}, bf16[2,64,3072]{2,1,0:T(8,128)(2,1)}, u32[]{:S(2)}, u32[]{:S(2)}) collective-permute-start(bf16[2,64,3072]{2,1,0:T(8,128)(2,1)S(1)} %shard_map.58.refs_0_), channel_id=1, source_target_pairs={{0,12},{4,0},{8,4},{12,8},{1,13},{5,1},{9,5},{13,9},{2,14},{6,2},{... | collective-permute-start | bytes 2359304 | tf_op jit(solution)/shard_map/ppermute | solution.py:162
  53.4 33.8 %collective-permute-start.6 = (bf16[2,64,3072]{2,1,0:T(8,128)(2,1)S(1)}, bf16[2,64,3072]{2,1,0:T(8,128)(2,1)}, u32[]{:S(2)}, u32[]{:S(2)}) collective-permute-start(bf16[2,64,3072]{2,1,0:T(8,128)(2,1)S(1)} %shard_map.58.refs_0_), channel_id=1, source_target_pairs={{0,8},{4,12},{8,0},{12,4},{1,9},{5,13},{9,1},{13,5},{2,10},{6,14},... | collective-permute-start | bytes 2359304 | tf_op jit(solution)/shard_map/ppermute | solution.py:162
  55.7 37.6 %collective-permute-start.5 = (bf16[2,64,3072]{2,1,0:T(8,128)(2,1)S(1)}, bf16[2,64,3072]{2,1,0:T(8,128)(2,1)}, u32[]{:S(2)}, u32[]{:S(2)}) collective-permute-start(bf16[2,64,3072]{2,1,0:T(8,128)(2,1)S(1)} %shard_map.58.refs_0_), channel_id=1, source_target_pairs={{0,4},{4,8},{8,12},{12,0},{1,5},{5,9},{9,13},{13,1},{2,6},{6,10},{... | collective-permute-start | bytes 2359304 | tf_op jit(solution)/shard_map/ppermute | solution.py:162
  58.5 53.8 %copy-start.5 = (bf16[2,64,3072]{2,1,0:T(8,128)(2,1)}, bf16[2,64,3072]{2,1,0:T(8,128)(2,1)S(1)}, u32[]{:S(2)}) copy-start(bf16[2,64,3072]{2,1,0:T(8,128)(2,1)S(1)} %collective-permute-done.9.refs_6_) | copy-start | bytes 2359300
  58.5 53.8 %collective-permute-start.13 = (bf16[4,64,3072]{2,1,0:T(8,128)(2,1)S(1)}, bf16[4,64,3072]{2,1,0:T(8,128)(2,1)}, u32[]{:S(2)}, u32[]{:S(2)}) collective-permute-start(bf16[4,64,3072]{2,1,0:T(8,128)(2,1)S(1)} %shard_map.57.refs_1_.refs_4_), channel_id=1, source_target_pairs={{0,1},{1,0},{2,3},{3,2},{4,5},{5,4},{6,7},{7,6},{8,9},{9,8},{10,11... | collective-permute-start | bytes 4718600 | tf_op jit(solution)/shard_map/ppermute | solution.py:192
  81.8 30.5 %collective-permute-start.14 = (bf16[4,64,3072]{2,1,0:T(8,128)(2,1)}, bf16[4,64,3072]{2,1,0:T(8,128)(2,1)}, u32[]{:S(2)}, u32[]{:S(2)}) collective-permute-start(bf16[4,64,3072]{2,1,0:T(8,128)(2,1)} %collective-permute-done.8.refs_5_), channel_id=1, source_target_pairs={{0,1},{1,0},{2,3},{3,2},{4,5},{5,4},{6,7},{7,6},{8,9},{9,8},{10,11... | collective-permute-start | bytes 4718600 | tf_op jit(solution)/shard_map/ppermute | solution.py:192
  85.3 26.9 %collective-permute-start.12 = (bf16[2,64,3072]{2,1,0:T(8,128)(2,1)}, bf16[2,64,3072]{2,1,0:T(8,128)(2,1)}, u32[]{:S(2)}, u32[]{:S(2)}) collective-permute-start(bf16[2,64,3072]{2,1,0:T(8,128)(2,1)} %collective-permute-done.7.refs_3_), channel_id=1, source_target_pairs={{0,1},{1,0},{2,3},{3,2},{4,5},{5,4},{6,7},{7,6},{8,9},{9,8},{10,11... | collective-permute-start | bytes 2359304 | tf_op jit(solution)/shard_map/ppermute | solution.py:192
  87.2 25.0 %collective-permute-start.11 = (bf16[2,64,3072]{2,1,0:T(8,128)(2,1)}, bf16[2,64,3072]{2,1,0:T(8,128)(2,1)}, u32[]{:S(2)}, u32[]{:S(2)}) collective-permute-start(bf16[2,64,3072]{2,1,0:T(8,128)(2,1)} %collective-permute-done.6.refs_2_), channel_id=1, source_target_pairs={{0,1},{1,0},{2,3},{3,2},{4,5},{5,4},{6,7},{7,6},{8,9},{9,8},{10,11... | collective-permute-start | bytes 2359304 | tf_op jit(solution)/shard_map/ppermute | solution.py:192
  93.3 18.9 %collective-permute-start.10 = (bf16[2,64,3072]{2,1,0:T(8,128)(2,1)}, bf16[2,64,3072]{2,1,0:T(8,128)(2,1)}, u32[]{:S(2)}, u32[]{:S(2)}) collective-permute-start(bf16[2,64,3072]{2,1,0:T(8,128)(2,1)} %collective-permute-done.5.refs_1_), channel_id=1, source_target_pairs={{0,1},{1,0},{2,3},{3,2},{4,5},{5,4},{6,7},{7,6},{8,9},{9,8},{10,11... | collective-permute-start | bytes 2359304 | tf_op jit(solution)/shard_map/ppermute | solution.py:192
  96.3 10.3 %all-to-all-start = ((s32[16,1,128]{2,1,0:T(1,128)}), s32[16,1,128]{2,1,0:T(1,128)S(1)}, u32[]{:S(2)}, u32[]{:S(2)}) async-start(s32[16,1,128]{2,1,0:T(1,128)} %broadcast_in_dim.2), calls=%async_computation | async-start | bytes 16384 | tf_op jit(solution)/shard_map/all_to_all | solution.py:184
  (1 other events, 0.5 us)
Sparse Core Ops, SparseCore 0:
  14.1 72.0 all-gather.1
